TPU v7x, 32 devices: a whole 2x2x4 slice. The times are simulated.
32 devices in a mesh: seq: 4 (over z), fsdp: 8 (over y, x, core).
Axes of the slice: x: 2, y: 2, z: 4, core: 2. Of those that a mesh axis runs over, the one named last changes fastest.
Arguments:
- inputs: bfloat16 [2, 8192, 1024], P(None, ('seq', 'fsdp')), may hold values from -6 to 6
- cotangent: bfloat16 [2, 8192, 1024], P(None, ('seq', 'fsdp')), may hold values from -6 to 6
- segment_ids: int32 [2, 8192], replicated, may hold values from 0 to 3, as said below
- norm1_gain: bfloat16 [1024], P('fsdp'), may hold values from 0.099609375 to 1.8984375
- norm1_bias: bfloat16 [1024], P('fsdp'), may hold values from -3 to 3
- qkv_weight: bfloat16 [1024, 3072], P(None, 'fsdp'), may hold values from -0.1875 to 0.1875
- qv_bias: bfloat16 [16, 128], P('fsdp'), may hold values from -3 to 3
- out_weight: bfloat16 [1024, 1024], P('fsdp'), may hold values from -1.5 to 1.5
- out_bias: bfloat16 [1024], P('fsdp'), may hold values from -3 to 3
- norm2_gain: bfloat16 [1024], P('fsdp'), may hold values from 0.099609375 to 1.8984375
- norm2_bias: bfloat16 [1024], P('fsdp'), may hold values from -3 to 3
- fc_weight: bfloat16 [1024, 4096], P(None, 'fsdp'), may hold values from -0.1875 to 0.1875
- fc_bias: bfloat16 [4096], P('fsdp'), may hold values from -3 to 3
- proj_weight: bfloat16 [4096, 1024], P('fsdp'), may hold values from -0.09375 to 0.09375
- proj_bias: bfloat16 [1024], P('fsdp'), may hold values from -3 to 3
Outputs:
- layer_output: bfloat16 [2, 8192, 1024], P(None, ('seq', 'fsdp'))
- input_grad: bfloat16 [2, 8192, 1024], P(None, ('seq', 'fsdp'))
- norm1_gain_grad: float32 [1024], P('fsdp')
- norm1_bias_grad: float32 [1024], P('fsdp')
- qkv_weight_grad: float32 [1024, 3072], P(None, 'fsdp')
- qv_bias_grad: float32 [16, 128], P('fsdp')
- out_weight_grad: float32 [1024, 1024], P('fsdp')
- out_bias_grad: float32 [1024], P('fsdp')
- norm2_gain_grad: float32 [1024], P('fsdp')
- norm2_bias_grad: float32 [1024], P('fsdp')
- fc_weight_grad: float32 [1024, 4096], P(None, 'fsdp')
- fc_bias_grad: float32 [4096], P('fsdp')
- proj_weight_grad: float32 [4096, 1024], P('fsdp')
- proj_bias_grad: float32 [1024], P('fsdp')
Inputs may be any that keep to these rules, and one draw needn't show every extreme that they name: `segment_ids`: along each sequence the ids start at 0 and never fall, rising by at most one from a token to the next. In every draw one sequence, chosen by the seed, is a single document; every other sequence holds exactly 4 documents.
All inputs are finite; a program needn't handle non-finite values.
Results may differ from a plain program's by a relative error of at most 0.012.
The roundings to bfloat16 on the way count: a program that leaves them out, or rounds other values in their place, can miss the bound.
Values may be sent and summed in bfloat16 or wider, within the bound.
A program may use at most 256 MiB of HBM per device.

v0:
```python
import functools
import math

import jax
import jax.numpy as jnp
from jax import lax
from jax.experimental import pallas as pl
from jax.experimental.pallas import tpu as pltpu
from jax.sharding import PartitionSpec as P


def standardize(values):
    centre = values - jnp.mean(values, axis=-1, keepdims=True)
    spread = jnp.mean(centre * centre, axis=-1, keepdims=True)
    rate = lax.rsqrt(spread + norm_eps)
    return centre * rate, rate


def norm_grad(direction, z, rate):
    mean_d = jnp.mean(direction, axis=-1, keepdims=True)
    mean_dz = jnp.mean(direction * z, axis=-1, keepdims=True)
    return rate * (direction - mean_d - z * mean_dz)


norm_eps = 1e-05

HD = 64
WINDOW = 1024
BLK = 256
PENALTY = 1e30


def nt(a, b):
    return lax.dot_general(a, b, (((1,), (1,)), ((), ())), preferred_element_type=jnp.float32)


def nn(a, b):
    return lax.dot_general(a, b, (((1,), (0,)), ((), ())), preferred_element_type=jnp.float32)


def tn(a, b):
    return lax.dot_general(a, b, (((0,), (0,)), ((), ())), preferred_element_type=jnp.float32)


def split3(v):
    hi = v.astype(jnp.bfloat16).astype(jnp.float32)
    rest = v - hi
    mid = rest.astype(jnp.bfloat16).astype(jnp.float32)
    return hi, mid, rest - mid


def merge_edges(mask, tiles):
    return [jnp.where(mask, tiles[0], tiles[-1])] + tiles[1:-1]


def spread_edges(mask, tiles):
    zero = jnp.zeros_like(tiles[0])
    return [jnp.where(mask, tiles[0], zero)] + tiles[1:] + [jnp.where(mask, zero, tiles[0])]


def edge_mask():
    rows = lax.broadcasted_iota(jnp.int32, (BLK, BLK), 0)
    cols = lax.broadcasted_iota(jnp.int32, (BLK, BLK), 1)
    return rows > cols


def xor(a, b, size):
    total, bit = 0, 1
    while bit < size:
        total = total + bit * lax.rem(lax.div(a, bit) + lax.div(b, bit), 2)
        bit *= 2
    return total


MESH = pl.DeviceIdType.MESH
SLOT_AT = (3, 2, 5, 4, 1, 0, 7, 6)
STEP_OF = tuple(SLOT_AT.index(r) for r in range(8))
NEAR = 6


def enter(peers):
    barrier = pltpu.get_barrier_semaphore()
    for peer in peers:
        pl.semaphore_signal(barrier, inc=1, device_id={"fsdp": peer}, device_id_type=MESH)
    pl.semaphore_wait(barrier, len(peers))


def attend_kernel(
    heads, group, qkv_ref, augk_ref, augq_ref, out_w, fc_w, proj_w,
    out_ref, q2_ref, halo_ref, merged_ref, out_all, fc_all, proj_all,
    keys, values, values_t, sent, behind, own_sems, send_sems, recv_sems, halo_sems, w_own, w_send, w_recv,
):
    step = pl.program_id(0)
    last = pl.num_programs(0) - 1
    me = lax.axis_index("fsdp")
    line = lax.axis_index("seq")
    line_end = lax.axis_size("seq") - 1
    at = [xor(me, k, group) for k in range(group)]
    seqs, rows = qkv_ref.shape[0], qkv_ref.shape[1]
    half = group // 2
    seq = lax.rem(lax.div(step, half), 2)
    lower = lax.div(step, group)
    place = (1 - lower) * half + lax.rem(step + me, half)
    width = heads * 2 * HD
    low = jnp.bfloat16

    def halo_copy():
        return pltpu.make_async_remote_copy(
            src_ref=qkv_ref.at[:, pl.ds(rows - WINDOW, WINDOW), pl.ds(0, width)],
            dst_ref=behind, send_sem=halo_sems.at[0], recv_sem=halo_sems.at[1],
            device_id={"seq": lax.rem(line + 1, line_end + 1)}, device_id_type=MESH,
        )

    weights = ((out_w, out_all, False), (fc_w, fc_all, True), (proj_w, proj_all, True))

    def slot(a, r):
        return weights[a][1].at[STEP_OF[r] if weights[a][2] else r]

    def w_copy(a, r, second=False):
        to = at[1] if r % 2 else at[r]
        src = weights[a][0] if r in (1, 2, 4) else slot(a, r - 1) if r % 2 else None
        dst, sem = slot(a, r), r
        if r == 6:
            size = weights[a][0].shape[0] // 2
            part = pl.ds(size if second else 0, size)
            src = slot(a, 4 if second else 2).at[part]
            to = at[2] if second else at[4]
            dst, sem = dst.at[part], 0 if second else 6
        return pltpu.make_async_remote_copy(
            src_ref=src, dst_ref=dst, send_sem=w_send.at[a, sem], recv_sem=w_recv.at[a, sem],
            device_id={"fsdp": to}, device_id_type=MESH,
        )

    def w_keep(a):
        return pltpu.make_async_copy(weights[a][0], slot(a, 0), w_own.at[a])

    even = lax.rem(line, 2)
    partner = line + 1 - 2 * even
    p_size = proj_w.shape[0] // 2
    p_part = pl.ds(pl.multiple_of(even * p_size, p_size), p_size)

    def p_near(r):
        return pltpu.make_async_remote_copy(
            src_ref=proj_w.at[p_part], dst_ref=slot(2, r).at[p_part], send_sem=w_send.at[2, r],
            recv_sem=w_recv.at[2, r], device_id={"fsdp": at[r]}, device_id_type=MESH,
        )

    def p_line(r):
        sem = 5 + r // 2
        return pltpu.make_async_remote_copy(
            src_ref=slot(2, r).at[p_part], dst_ref=slot(2, r).at[p_part], send_sem=w_send.at[2, sem],
            recv_sem=w_recv.at[2, sem], device_id={"seq": partner}, device_id_type=MESH,
        )

    def forward(a):
        w_copy(a, 2).wait_recv()
        w_copy(a, 3).start()
        w_copy(a, 4).wait_recv()
        w_copy(a, 5).start()
        if not weights[a][2]:
            w_copy(a, 6).start()
            w_copy(a, 6, True).start()

    @pl.when(step == 0)
    def _():
        barrier = pltpu.get_barrier_semaphore()
        for peer in at[1:]:
            pl.semaphore_signal(barrier, inc=1, device_id={"fsdp": peer}, device_id_type=MESH)

        pl.semaphore_signal(
            barrier, inc=1, device_id={"seq": lax.rem(line + line_end, line_end + 1)}, device_id_type=MESH
        )
        pl.semaphore_signal(barrier, inc=1, device_id={"seq": partner}, device_id_type=MESH)
        pl.semaphore_wait(barrier, group + 1)

        @pl.when(line < line_end)
        def _():
            halo_copy().start()

        for r in (2, 4, 1):
            w_copy(0, r).start()
        for r in (2, 4):
            p_near(r).start()
        w_copy(2, 1).start()
        w_keep(0).start()
        for s in range(seqs):
            fill_keys(s, heads, qkv_ref, augk_ref, WINDOW, keys, values, values_t, None)

    @pl.when(step == group)
    def _():
        @pl.when(line > 0)
        def _():
            halo_copy().wait_recv()

        @pl.when(line == 0)
        def _():
            behind[...] = jnp.zeros_like(behind)

        halo_ref[...] = behind[...]
        for s in range(seqs):
            fill_keys(s, heads, behind, augk_ref, 0, keys, values, values_t, None)

    mask = edge_mask()
    tiles = WINDOW // BLK + 1
    start = pl.multiple_of(place * BLK, BLK)
    lane = lax.broadcasted_iota(jnp.int32, (BLK, 2 * HD), 1)
    lse_lane = augq_ref.shape[2] + HD - 3
    slot_k = xor(me, place, group)
    spans = [pl.ds(pl.multiple_of(start + b * BLK, BLK), BLK) for b in range(tiles)]
    for h in range(heads):
        sh = seq * heads + h
        qc = heads * 2 * HD + h * HD
        q = jnp.concatenate(
            [qkv_ref[seq, pl.ds(start, BLK), qc : qc + HD] * 0.125, augq_ref[seq, pl.ds(start, BLK), :]], axis=1
        )
        scores = merge_edges(mask, [nt(keys[sh, s, :], q) for s in spans])
        peak = functools.reduce(jnp.maximum, scores)
        peak = jnp.max(peak, axis=0, keepdims=True)
        weights_ = spread_edges(mask, [jnp.exp(s - peak).astype(low) for s in scores])
        total = sum(nn(values_t[sh, :, s], w) for s, w in zip(spans, weights_))
        sub = lax.broadcasted_iota(jnp.int32, total.shape, 0)
        total = jnp.where(sub == HD + 1, peak, total).T
        norm = total[:, HD : HD + 1]
        part = (total[:, :HD] / norm).astype(low)
        out_ref[seq, pl.ds(start, BLK), h * HD : (h + 1) * HD] = part
        sent[step, :, h * HD : (h + 1) * HD] = part
        lse = total[:, HD + 1 : HD + 2] + jnp.log(norm)
        hi, mid, lo = split3(-lse)
        q2 = q.astype(jnp.float32)
        q2 = jnp.where(lane == lse_lane, hi, q2)
        q2 = jnp.where(lane == lse_lane + 1, mid, q2)
        q2 = jnp.where(lane == lse_lane + 2, lo, q2)
        q2_ref[seq, h, pl.ds(start, BLK), :] = q2.astype(low)

    span = sent.shape[2]

    def landing(s, k):
        return merged_ref.at[s, :, pl.ds(pl.multiple_of(k * span, span), span)]

    def own(s):
        return pltpu.make_async_copy(sent.at[step], landing(s, 0), own_sems.at[s])

    def away(s, k, to):
        return pltpu.make_async_remote_copy(
            src_ref=sent.at[step], dst_ref=landing(s, k), send_sem=send_sems.at[s, k], recv_sem=recv_sems.at[s, k],
            device_id={"fsdp": to}, device_id_type=MESH,
        )

    @pl.when(place == me)
    def _():
        own(seq).start()

    @pl.when(place != me)
    def _():
        away(seq, slot_k, place).start()

    @pl.when(step == 3)
    def _():
        forward(0)
        for r in (2, 4, 1):
            w_copy(1, r).start()

    @pl.when(step == 6)
    def _():
        for r in (2, 4):
            p_near(r).wait_recv()
            p_line(r).start()

    @pl.when(step == 10)
    def _():
        w_copy(0, 6).wait_recv()
        w_copy(0, 6, True).wait_recv()
        w_copy(0, 7).start()

    @pl.when(step == last)
    def _():
        forward(1)
        for r in (2, 4):
            p_line(r).wait_recv()
            w_copy(2, r + 1).start()
        for s in range(seqs):
            own(s).wait()
            for k in range(1, group):
                away(s, k, at[k]).wait()
        w_keep(0).wait()
        for a in range(2):
            for r in (1, 2, 3, 4, 5):
                w_copy(a, r).wait_send()
            for r in (1, 3, 5):
                w_copy(a, r).wait_recv()
        for r in (2, 4):
            p_near(r).wait_send()
            p_line(r).wait_send()
        for r in (1, 3, 5):
            w_copy(2, r).wait()
        w_copy(0, 6).wait_send()
        w_copy(0, 6, True).wait_send()
        w_copy(0, 7).wait()

        @pl.when(line < line_end)
        def _():
            halo_copy().wait_send()


def fill_keys(s, heads, source, augk_ref, base, keys, values, values_t, keys_t):
    size = BLK
    ones = jnp.ones((size, HD), jnp.bfloat16)
    first = source.shape[1] - WINDOW if base == 0 else 0
    for h in range(heads):
        c = h * 2 * HD
        for i in range(source.shape[1] // size):
            pair = source[s, i * size : (i + 1) * size, c : c + 2 * HD]
            span = slice(base + i * size, base + (i + 1) * size)
            k = jnp.concatenate([pair[:, :HD], augk_ref[s, span, :]], axis=1)
            v = jnp.concatenate([pair[:, HD:], ones], axis=1)
            keys[s * heads + h, span, :] = k
            values[s * heads + h, span, :] = v
            if values_t is not None:
                values_t[s * heads + h, :, span] = v.T
            if keys_t is not None:
                keys_t[s * heads + h, :, span] = k.T


def attend(qkv, augk, augq, out_w, fc_w, proj_w, heads, group):
    seqs, rows, cols = qkv.shape
    ext = augk.shape[1]
    assert rows // BLK == group
    low = jnp.bfloat16
    vmem = pl.BlockSpec(memory_space=pltpu.VMEM)
    hbm = pl.BlockSpec(memory_space=pl.ANY)
    every = seqs * heads
    return pl.pallas_call(
        functools.partial(attend_kernel, heads, group),
        grid=(seqs * rows // BLK,),
        in_specs=[vmem] * 3 + [hbm] * 3,
        out_specs=[vmem] * 3 + [hbm] * 4,
        out_shape=[
            jax.ShapeDtypeStruct((seqs, rows, heads * HD), low),
            jax.ShapeDtypeStruct((seqs, heads, rows, 2 * HD), low),
            jax.ShapeDtypeStruct((seqs, WINDOW, heads * 2 * HD), low),
            jax.ShapeDtypeStruct((seqs, BLK, group * heads * HD), low),
        ]
        + [jax.ShapeDtypeStruct((n,) + w.shape, low) for n, w in ((group, out_w), (NEAR - 1, fc_w), (NEAR - 1, proj_w))],
        scratch_shapes=[
            pltpu.VMEM((every, ext, 2 * HD), low),
            pltpu.VMEM((every, ext, 2 * HD), low),
            pltpu.VMEM((every, 2 * HD, ext), low),
            pltpu.VMEM((seqs * rows // BLK, BLK, heads * HD), low),
            pltpu.VMEM((seqs, WINDOW, heads * 2 * HD), low),
            pltpu.SemaphoreType.DMA((seqs,)),
            pltpu.SemaphoreType.DMA((seqs, group)),
            pltpu.SemaphoreType.DMA((seqs, group)),
            pltpu.SemaphoreType.DMA((2,)),
            pltpu.SemaphoreType.DMA((1,)),
            pltpu.SemaphoreType.DMA((3, group)),
            pltpu.SemaphoreType.DMA((3, group)),
        ],
        compiler_params=pltpu.CompilerParams(vmem_limit_bytes=56 * 2**20, collective_id=1, has_side_effects=True),
        name="attend",
    )(qkv, augk, augq, out_w, fc_w, proj_w)


def mask_features(segment_ext, docs):
    doc = jnp.arange(docs, dtype=jnp.int32)
    hot = (segment_ext[..., None] == doc).astype(jnp.bfloat16)
    rows = segment_ext.shape[1]
    outside = (segment_ext < 0).astype(jnp.bfloat16)[..., None]
    pad = HD - docs - 4
    one = jnp.ones(segment_ext.shape + (3,), jnp.bfloat16)
    zero = jnp.zeros(segment_ext.shape + (pad,), jnp.bfloat16)
    keys = jnp.concatenate([-hot, -outside, zero, one], axis=-1)
    own = hot[:, WINDOW:]
    queries = jnp.concatenate(
        [
            (1 - own) * jnp.bfloat16(PENALTY),
            jnp.full(own.shape[:2] + (1,), PENALTY, jnp.bfloat16),
            jnp.zeros(own.shape[:2] + (pad + 3,), jnp.bfloat16),
        ],
        axis=-1,
    )
    return keys, queries


def gather_project_kernel(
    x_ref, *rest,
):
    parts, rest = rest[:7], rest[7:]
    project_kernel(x_ref, parts, *rest)


def project_kernel(
    x_ref, parts, w_ref, b_ref, all_small_ref, pieces_out, qkv_ref,
    z1, pieces, smalls, small_ref, small_send, small_recv, send_sems, recv_sems, out_sems,
):
    group = all_small_ref.shape[0]
    me = lax.axis_index("fsdp")
    at = [xor(me, k, group) for k in range(group)]
    rows = x_ref.shape[0] // 2
    f32, low = jnp.float32, jnp.bfloat16
    enter(at[1:])

    def small_copy(k):
        return pltpu.make_async_remote_copy(
            src_ref=small_ref, dst_ref=smalls.at[me], send_sem=small_send.at[k], recv_sem=small_recv.at[k],
            device_id={"fsdp": at[k]}, device_id_type=MESH,
        )

    row = 0
    small_ref[...] = jnp.zeros_like(small_ref)
    for part in parts:
        small_ref[row : row + part.shape[0], :] = part[...]
        row += part.shape[0]
    for k in range(1, group):
        small_copy(k).start()
    smalls[me] = small_ref[...]

    def chunk(p, s):
        return pieces.at[p, s]

    def move(r, s):
        if r % 2:
            piece, to = at[r - 1], at[1]
        elif r == 6:
            piece, to = (at[2], at[4]) if s == 0 else (at[4], at[2])
        else:
            piece, to = me, at[r]
        return pltpu.make_async_remote_copy(
            src_ref=chunk(piece, s), dst_ref=chunk(piece, s), send_sem=send_sems.at[r, s], recv_sem=recv_sems.at[r, s],
            device_id={"fsdp": to}, device_id_type=MESH,
        )

    def keep(k, s):
        return pltpu.make_async_copy(chunk(at[k], s), pieces_out.at[s, pl.ds(pl.multiple_of(at[k] * rows, rows), rows)], out_sems.at[k, s])

    def project(k, s):
        keep(k, s).start()
        start = pl.multiple_of(at[k] * rows, rows)
        qkv_ref[s, pl.ds(start, rows), :] = (nn(pieces[at[k], s], w_ref[...]) + b_ref[...]).astype(low)

    for s in range(2):
        z1[s * rows : (s + 1) * rows, :] = standardize(x_ref[s * rows : (s + 1) * rows, :].astype(f32))[0]
    for k in range(1, group):
        small_copy(k).wait()
    gain = jnp.concatenate([smalls[f, 0:1, :] for f in range(group)], axis=1).astype(f32)
    offset = jnp.concatenate([smalls[f, 1:2, :] for f in range(group)], axis=1).astype(f32)
    for s in range(2):
        pieces[me, s] = (z1[s * rows : (s + 1) * rows, :] * gain + offset).astype(low)
        move(2, s).start()
        move(4, s).start()
        move(1, s).start()
    all_small_ref[...] = smalls[...]
    for s in range(2):
        project(0, s)
    for s in range(2):
        move(1, s).wait_recv()
        project(1, s)
    for s in range(2):
        move(2, s).wait_recv()
        if s == 0:
            move(6, 0).start()
        move(3, s).start()
        move(4, s).wait_recv()
        if s == 1:
            move(6, 1).start()
        move(5, s).start()
        project(2, s)
        project(4, s)
    for s in range(2):
        move(3, s).wait_recv()
        project(3, s)
        move(5, s).wait_recv()
        project(5, s)
    for s in range(2):
        move(6, s).wait_recv()
        move(7, s).start()
        project(6, s)
    for s in range(2):
        move(7, s).wait_recv()
        project(7, s)
    for s in range(2):
        for r in range(1, group):
            move(r, s).wait_send()
        for k in range(group):
            keep(k, s).wait()


def gather_project(x, smalls, weight, bias, group):
    rows, width = x.shape
    cols = weight.shape[1]
    half = rows // 2
    span = smalls[0].shape[1]
    vmem = pl.BlockSpec(memory_space=pltpu.VMEM)
    low = jnp.bfloat16
    return pl.pallas_call(
        gather_project_kernel,
        in_specs=[vmem] * 10,
        out_specs=[vmem, pl.BlockSpec(memory_space=pl.ANY), vmem],
        out_shape=[
            jax.ShapeDtypeStruct((group, 16, span), low),
            jax.ShapeDtypeStruct((2, group * half, width), low),
            jax.ShapeDtypeStruct((2, group * half, cols), low),
        ],
        scratch_shapes=[
            pltpu.VMEM((rows, width), jnp.float32),
            pltpu.VMEM((group, 2, half, width), low),
            pltpu.VMEM((group, 16, span), low),
            pltpu.VMEM((16, span), low),
            pltpu.SemaphoreType.DMA((group,)),
            pltpu.SemaphoreType.DMA((group,)),
            pltpu.SemaphoreType.DMA((group, 2)),
            pltpu.SemaphoreType.DMA((group, 2)),
            pltpu.SemaphoreType.DMA((group, 2)),
        ],
        compiler_params=pltpu.CompilerParams(
            vmem_limit_bytes=48 * 2**20, collective_id=2, has_side_effects=True
        ),
        name="gather_project",
    )(x, *smalls, weight, bias)


def gelu_both(v):
    c = math.sqrt(2.0 / math.pi)
    square = v * v
    t = jnp.tanh(v * (c + (c * 0.044715) * square))
    half = 0.5 * (1.0 + t)
    slope = half + (0.5 * v) * (1.0 - t * t) * (c + (3.0 * 0.044715 * c) * square)
    return v * half, slope


def column_sums(array):
    return jnp.sum(array, axis=0, keepdims=True)


def feed_forward_kernel(
    group, x_ref, cot_ref, merged_ref, out_ref, fc_near, proj_near, fc_own, proj_own, fcb_ref, vec_ref,
    layer_ref, gres_ref, gheads_ref, keep_ref, side_ref, gout_ref, gvec_ref, gfcb_ref,
    resid, z2, rate, normed, total, gnormed, fc_w, proj_w, given, taken, gmerged, gout_given, gout_taken,
    load_sems, far_send, far_recv, pair_send, pair_recv, side_send, side_recv, keep_sems, head_send, head_recv,
    own_sem, gout_sems,
):
    step = pl.program_id(0)
    last = group - 1
    me = lax.axis_index("fsdp")
    at = [xor(me, k, group) for k in range(group)]
    rows = x_ref.shape[0]
    block = rows // 2
    f32, low = jnp.float32, jnp.bfloat16
    span = merged_ref.shape[1] // group

    def load(a, i):
        near, here = ((fc_near, fc_w), (proj_near, proj_w))[a]
        return pltpu.make_async_copy(near.at[i], here.at[lax.rem(i, 2)], load_sems.at[a, lax.rem(i, 2)])

    def load_own(a):
        i = (NEAR - 1) % 2
        return pltpu.make_async_copy((fc_own, proj_own)[a], (fc_w, proj_w)[a].at[i], load_sems.at[a, i])

    def far_copy(a, way):
        near, here = ((fc_near, fc_w), (proj_near, proj_w))[a]
        size = near.shape[1] // 2
        if way == 2:
            src, dst, to = here.at[3], here.at[2], at[1]
        else:
            part = pl.ds(way * size, size)
            src, dst = near.at[STEP_OF[(2, 4)[way]], part], here.at[3, part]
            to = at[(4, 2)[way]]
        return pltpu.make_async_remote_copy(
            src_ref=src, dst_ref=dst, send_sem=far_send.at[a, way], recv_sem=far_recv.at[a, way],
            device_id={"fsdp": to}, device_id_type=MESH,
        )

    def pair_copy(j):
        return pltpu.make_async_remote_copy(
            src_ref=given.at[lax.rem(j, 2)], dst_ref=taken.at[j], send_sem=pair_send.at[j], recv_sem=pair_recv.at[j],
            device_id={"fsdp": at[1]}, device_id_type=MESH,
        )

    def side_copy(a):
        return pltpu.make_async_remote_copy(
            src_ref=taken.at[a, a], dst_ref=side_ref.at[a], send_sem=side_send.at[a], recv_sem=side_recv.at[a],
            device_id={"fsdp": at[(2, 4)[a]]}, device_id_type=MESH,
        )

    def keep_copy(j):
        return pltpu.make_async_copy(taken.at[j], keep_ref.at[j], keep_sems.at[j])

    def head_copy(k):
        src = gmerged.at[:, :, pl.ds(k * span, span)]
        dst = gheads_ref.at[:, pl.ds(pl.multiple_of(me * block, block), block), :]
        if k == 0:
            return pltpu.make_async_copy(src, dst, own_sem)
        return pltpu.make_async_remote_copy(
            src_ref=src, dst_ref=dst, send_sem=head_send.at[k], recv_sem=head_recv.at[k],
            device_id={"fsdp": at[k]}, device_id_type=MESH,
        )

    def gout_copy():
        return pltpu.make_async_remote_copy(
            src_ref=gout_given, dst_ref=gout_taken, send_sem=gout_sems.at[0], recv_sem=gout_sems.at[1],
            device_id={"fsdp": at[1]}, device_id_type=MESH,
        )

    @pl.when(step == 0)
    def _():
        enter(at[1:])
        for a in range(2):
            load(a, 0).start()
        for a in range(2):
            far_copy(a, 0).start()
            far_copy(a, 1).start()
        acc = x_ref[...].astype(f32) + vec_ref[0:1, :] + nn(merged_ref[...], out_ref[...])
        resid[...] = acc
        z, r = standardize(acc)
        z2[...] = z
        rate[...] = jnp.broadcast_to(r, rate.shape)
        normed[...] = (z * vec_ref[1:2, :] + vec_ref[2:3, :]).astype(low)
        total[...] = jnp.zeros_like(total)
        gnormed[...] = jnp.zeros_like(gnormed)

    j = lax.div(step, 2)
    odd = lax.rem(step, 2)

    @pl.when(step < NEAR - 1)
    def _():
        for a in range(2):
            load(a, step).wait()

    @pl.when(step == NEAR - 1)
    def _():
        for a in range(2):
            load_own(a).wait()

    @pl.when(step + 1 < NEAR - 1)
    def _():
        for a in range(2):
            load(a, step + 1).start()

    @pl.when(step + 1 == NEAR - 1)
    def _():
        for a in range(2):
            load_own(a).start()

    @pl.when(step == NEAR)
    def _():
        for a in range(2):
            far_copy(a, 2).wait_recv()

    @pl.when((odd == 0) & (j >= 2))
    def _():
        pair_copy(j - 2).wait_send()

    here = jnp.where(step < NEAR, lax.rem(step, 2), step - NEAR + 2)
    fresh = jnp.where(odd == 0, lax.rem(j, 2), 2)
    hidden = nn(normed[...], fc_w[here]) + fcb_ref[0]
    gactive = nt(cot_ref[...], proj_w[here])
    active, slope = gelu_both(hidden)
    active = active.astype(low)
    ghidden = gactive * slope
    gfcb_ref[0] = column_sums(ghidden)
    ghidden = ghidden.astype(low)
    total[...] += nn(active, proj_w[here])
    gnormed[...] += nt(ghidden, fc_w[here])
    given[fresh, 0] = tn(normed[...], ghidden).astype(low)
    gproj = tn(active, cot_ref[...]).astype(low)
    size, part = gproj.shape[0], fc_w.shape[2]
    for i in range(gproj.shape[1] // part):
        given[fresh, 1, i * size : (i + 1) * size, :] = gproj[:, i * part : (i + 1) * part]

    @pl.when(odd == 0)
    def _():
        pair_copy(j).start()

    @pl.when(odd == 1)
    def _():
        pair_copy(j).wait_recv()

        def add(i, _):
            part = pl.ds(pl.multiple_of(lax.rem(i, 8) * 128, 128), 128)
            a = lax.div(i, 8)
            taken[j, a, part, :] = (taken[j, a, part, :].astype(f32) + given[2, a, part, :].astype(f32)).astype(low)
            return 0

        lax.fori_loop(0, 16, add, 0)
        keep_copy(j).start()

    for a in range(2):
        @pl.when(step == 1 + 2 * a)
        def _(a=a):
            side_copy(a).start()

    @pl.when(step == 3)
    def _():
        for a in range(2):
            far_copy(a, 0).wait_recv()
            far_copy(a, 1).wait_recv()
            far_copy(a, 2).start()

    @pl.when(step == last)
    def _():
        cot32 = cot_ref[...].astype(f32)
        g, z = gnormed[...], z2[...]
        gres = cot32 + norm_grad(g * vec_ref[1:2, :], z, rate[:, :1])
        gres_ref[...] = gres
        gattn = gres.astype(low)
        back = nt(gattn, out_ref[...]).astype(low)
        for s in range(2):
            gmerged[s] = back[s * block : (s + 1) * block, :]
        for k in (6, 2, 4, 3, 5, 7, 1, 0):
            head_copy(k).start()
        gout = tn(merged_ref[...], gattn)
        for k in range(1, group, 2):
            gout_given[k // 2] = gout[k * span : (k + 1) * span, :].astype(low)
        gout_copy().start()
        layer_ref[...] = (resid[...] + total[...] + vec_ref[3:4, :]).astype(low)
        gvec_ref[0:1, :] = column_sums(gattn.astype(f32))
        gvec_ref[1:2, :] = column_sums(g * z)
        gvec_ref[2:3, :] = column_sums(g)
        gvec_ref[3:4, :] = column_sums(cot32)
        gout_copy().wait_recv()
        for k in range(0, group, 2):
            mine = gout[k * span : (k + 1) * span, :].astype(low).astype(f32)
            gout_ref[k // 2] = (mine + gout_taken[k // 2].astype(f32)).astype(low)
        for k in range(group):
            head_copy(k).wait()
        gout_copy().wait_send()
        for a in range(2):
            for way in range(3):
                far_copy(a, way).wait_send()
        pair_copy(2).wait_send()
        pair_copy(3).wait_send()
        side_copy(0).wait()
        side_copy(1).wait()
        for i in range(group // 2):
            keep_copy(i).wait()


def feed_forward(x, cot, merged, out_all, fc_near, proj_near, fc_own, proj_own, fc_bias, vectors):
    rows, width = x.shape
    group, part = fc_bias.shape[0], fc_near.shape[2]
    span = width // group
    f32, low = jnp.float32, jnp.bfloat16
    vmem = pl.BlockSpec(memory_space=pltpu.VMEM)
    hbm = pl.BlockSpec(memory_space=pl.ANY)
    return pl.pallas_call(
        functools.partial(feed_forward_kernel, group),
        grid=(group,),
        in_specs=[
            vmem, vmem, vmem, vmem,
            hbm, hbm, hbm, hbm,
            pl.BlockSpec((1, 1, part), lambda i: (i, 0, 0)),
            vmem,
        ],
        out_specs=[
            vmem, vmem, hbm,
            hbm, hbm, vmem, vmem,
            pl.BlockSpec((1, 1, part), lambda i: (i, 0, 0)),
        ],
        out_shape=[
            jax.ShapeDtypeStruct((rows, width), low),
            jax.ShapeDtypeStruct((rows, width), f32),
            jax.ShapeDtypeStruct((2, group * rows // 2, span), low),
            jax.ShapeDtypeStruct((group // 2, 2, width, part), low),
            jax.ShapeDtypeStruct((2, width, part), low),
            jax.ShapeDtypeStruct((group // 2, span, width), low),
            jax.ShapeDtypeStruct((8, width), f32),
            jax.ShapeDtypeStruct((group, 1, part), f32),
        ],
        scratch_shapes=[
            pltpu.VMEM((rows, width), f32),
            pltpu.VMEM((rows, width), f32),
            pltpu.VMEM((rows, 128), f32),
            pltpu.VMEM((rows, width), low),
            pltpu.VMEM((rows, width), f32),
            pltpu.VMEM((rows, width), f32),
            pltpu.VMEM((4, width, part), low),
            pltpu.VMEM((4, part, width), low),
            pltpu.VMEM((3, 2, width, part), low),
            pltpu.VMEM((group // 2, 2, width, part), low),
            pltpu.VMEM((2, rows // 2, width), low),
            pltpu.VMEM((group // 2, span, width), low),
            pltpu.VMEM((group // 2, span, width), low),
            pltpu.SemaphoreType.DMA((2, 2)),
            pltpu.SemaphoreType.DMA((2, 3)),
            pltpu.SemaphoreType.DMA((2, 3)),
            pltpu.SemaphoreType.DMA((group // 2,)),
            pltpu.SemaphoreType.DMA((group // 2,)),
            pltpu.SemaphoreType.DMA((2,)),
            pltpu.SemaphoreType.DMA((2,)),
            pltpu.SemaphoreType.DMA((group // 2,)),
            pltpu.SemaphoreType.DMA((group,)),
            pltpu.SemaphoreType.DMA((group,)),
            pltpu.SemaphoreType.DMA,
            pltpu.SemaphoreType.DMA((2,)),
        ],
        compiler_params=pltpu.CompilerParams(vmem_limit_bytes=62 * 2**20, collective_id=3, has_side_effects=True),
        name="feed_forward",
    )(x, cot, merged, out_all, fc_near, proj_near, fc_own, proj_own, fc_bias, vectors)


def attend_back_kernel(
    heads, group, qkv_ref, halo_ref, augk_ref, q2_ref, out_ref, grad_ref, kept, side,
    gqkv_ref, sums_ref,
    keys, values, keys_t, dkeys, dvalues, edge, ahead, mid, near, far, mine, met,
    edge_sems, load_sems, near_send, near_recv, far_send, far_recv,
):
    step = pl.program_id(0)
    last = pl.num_programs(0) - 1
    me = lax.axis_index("fsdp")
    line = lax.axis_index("seq")
    line_end = lax.axis_size("seq") - 1
    at = [xor(me, k, group) for k in range(group)]
    seqs, rows = qkv_ref.shape[0], qkv_ref.shape[1]
    half = group // 2
    seq = lax.rem(lax.div(step, half), 2)
    place = lax.div(step, group) * half + lax.rem(step, half)
    f32, low = jnp.float32, jnp.bfloat16
    pieces = 2
    size = mid.shape[1] // pieces

    def edge_copy(s):
        return pltpu.make_async_remote_copy(
            src_ref=edge.at[s], dst_ref=ahead.at[s], send_sem=edge_sems.at[0, s], recv_sem=edge_sems.at[1, s],
            device_id={"seq": lax.rem(line + line_end, line_end + 1)}, device_id_type=MESH,
        )

    first, second = (at[2], at[4]), (at[4], at[2])

    def near_copy(a, h):
        part = pl.ds(h * size, size)
        return pltpu.make_async_remote_copy(
            src_ref=kept.at[3, a, part], dst_ref=near.at[a, part], send_sem=near_send.at[a, h],
            recv_sem=near_recv.at[a, h], device_id={"fsdp": first[a]}, device_id_type=MESH,
        )

    def far_copy(a, h):
        part = pl.ds(h * size, size)
        return pltpu.make_async_remote_copy(
            src_ref=mid.at[a, part], dst_ref=far.at[a, part], send_sem=far_send.at[a, h],
            recv_sem=far_recv.at[a, h], device_id={"fsdp": second[a]}, device_id_type=MESH,
        )

    def loads():
        for a in range(2):
            yield pltpu.make_async_copy(kept.at[1 - a, a], mid.at[a], load_sems.at[0, a])
            yield pltpu.make_async_copy(kept.at[2, a], mine.at[a], load_sems.at[1, a])
            yield pltpu.make_async_copy(side.at[a], met.at[a], load_sems.at[2, a])

    def plus(u, *more):
        total = u.astype(f32)
        for v in more:
            total += v.astype(f32)
        return total.astype(low)

    @pl.when(step == 0)
    def _():
        barrier = pltpu.get_barrier_semaphore()
        for peer in (at[2], at[4]):
            pl.semaphore_signal(barrier, inc=1, device_id={"fsdp": peer}, device_id_type=MESH)
        pl.semaphore_signal(
            barrier, inc=1, device_id={"seq": lax.rem(line + 1, line_end + 1)}, device_id_type=MESH
        )
        pl.semaphore_wait(barrier, 3)
        for h in range(pieces):
            for a in range(2):
                near_copy(a, h).start()
        for load in loads():
            load.start()
        for s in range(seqs):
            fill_keys(s, heads, halo_ref, augk_ref, 0, keys, values, None, keys_t)
            fill_keys(s, heads, qkv_ref, augk_ref, WINDOW, keys, values, None, keys_t)
        dkeys[...] = jnp.zeros_like(dkeys)
        dvalues[...] = jnp.zeros_like(dvalues)

    for s in range(seqs):
        @pl.when((step == (s + 1) * half) & (line > 0))
        def _(s=s):
            for h in range(heads):
                c = h * 2 * HD
                edge[s, :, c : c + 2 * HD] = jnp.concatenate(
                    [dkeys[s * heads + h, :WINDOW, :HD], dvalues[s * heads + h, :WINDOW, :HD]], axis=1
                ).astype(low)
            edge_copy(s).start()

    mask = edge_mask()
    tiles = WINDOW // BLK + 1
    start = pl.multiple_of(place * BLK, BLK)
    lane = lax.broadcasted_iota(jnp.int32, (BLK, 2 * HD), 1)
    spans = [pl.ds(pl.multiple_of(start + b * BLK, BLK), BLK) for b in range(tiles)]
    for h in range(heads):
        sh = seq * heads + h
        q = q2_ref[0, h]
        g32 = grad_ref[0, :, h * HD : (h + 1) * HD].astype(f32)
        centre = jnp.sum(g32 * out_ref[0, :, h * HD : (h + 1) * HD].astype(f32), axis=1, keepdims=True)
        hi, md, lo = split3(-centre)
        g2 = jnp.concatenate([g32, jnp.zeros((BLK, HD), f32)], axis=1)
        g2 = jnp.where(lane == HD, hi, g2)
        g2 = jnp.where(lane == HD + 1, md, g2)
        g2 = jnp.where(lane == HD + 2, lo, g2).astype(low)
        scores = merge_edges(mask, [nt(keys[sh, s, :], q) for s in spans])
        wgrads = merge_edges(mask, [nt(values[sh, s, :], g2) for s in spans])
        weights = [jnp.exp(s) for s in scores]
        sgrads = spread_edges(mask, [(w * d).astype(low) for w, d in zip(weights, wgrads)])
        weights = spread_edges(mask, [w.astype(low) for w in weights])
        for s, w, d in zip(spans, weights, sgrads):
            dvalues[sh, s, :] += nn(w, g2)
            dkeys[sh, s, :] += nn(d, q)
        dq = sum(nn(keys_t[sh, :, s], d) for s, d in zip(spans, sgrads))
        qc = heads * 2 * HD + h * HD
        gqkv_ref[seq, pl.ds(start, BLK), qc : qc + HD] = (dq.T[:, :HD] * 0.125).astype(low)

    def relay(h):
        part = slice(h * size, (h + 1) * size)
        for a in range(2):
            near_copy(a, h).wait_recv()
            mid[a, part] = plus(mid[a, part], near[a, part])
            far_copy(a, h).start()

    @pl.when(step == 4)
    def _():
        for load in loads():
            load.wait()
        relay(0)

    @pl.when(step == 8)
    def _():
        relay(1)

    @pl.when(step == last)
    def _():
        for s in range(seqs):
            for h in range(heads):
                c = h * 2 * HD
                own = jnp.concatenate(
                    [dkeys[s * heads + h, WINDOW:, :HD], dvalues[s * heads + h, WINDOW:, :HD]], axis=1
                )
                gqkv_ref[s, : rows - WINDOW, c : c + 2 * HD] = own[: rows - WINDOW].astype(low)
                dkeys[s * heads + h, WINDOW:, :] = own

        @pl.when(line < line_end)
        def _():
            for s in range(seqs):
                edge_copy(s).wait_recv()

        @pl.when(line == line_end)
        def _():
            ahead[...] = jnp.zeros_like(ahead)

        for s in range(seqs):
            for h in range(heads):
                c = h * 2 * HD
                own = dkeys[s * heads + h, rows:, :]
                gqkv_ref[s, rows - WINDOW :, c : c + 2 * HD] = (
                    own + ahead[s, :, c : c + 2 * HD].astype(f32)
                ).astype(low)

        for h in range(pieces):
            part = slice(h * size, (h + 1) * size)
            for a in range(2):
                far_copy(a, h).wait_recv()
                sums_ref[a, part] = plus(mine[a, part], met[a, part], far[a, part])
        for a in range(2):
            for h in range(pieces):
                near_copy(a, h).wait_send()
                far_copy(a, h).wait_send()

        @pl.when(line > 0)
        def _():
            for s in range(seqs):
                edge_copy(s).wait_send()


def attend_back(qkv, halo, augk, q2, out, grad, kept, side, heads, group):
    seqs, rows, cols = qkv.shape
    ext = augk.shape[1]
    half = group // 2
    f32, low = jnp.float32, jnp.bfloat16
    vmem = pl.BlockSpec(memory_space=pltpu.VMEM)
    hbm = pl.BlockSpec(memory_space=pl.ANY)
    every = seqs * heads
    part = kept.shape[2:]
    seq_of = lambda i: lax.rem(lax.div(i, half), 2)
    place_of = lambda i: lax.div(i, group) * half + lax.rem(i, half)
    edge = pltpu.VMEM((seqs, WINDOW, heads * 2 * HD), low)
    pair = pltpu.VMEM((2,) + part, low)
    return pl.pallas_call(
        functools.partial(attend_back_kernel, heads, group),
        grid=(seqs * rows // BLK,),
        in_specs=[
            vmem, vmem, vmem,
            pl.BlockSpec((1, heads, BLK, 2 * HD), lambda i: (seq_of(i), 0, place_of(i), 0)),
            pl.BlockSpec((1, BLK, heads * HD), lambda i: (seq_of(i), place_of(i), 0)),
            pl.BlockSpec((1, BLK, heads * HD), lambda i: (seq_of(i), place_of(i), 0)),
            hbm, hbm,
        ],
        out_specs=[vmem, vmem],
        out_shape=[
            jax.ShapeDtypeStruct((seqs, rows, cols), low),
            jax.ShapeDtypeStruct((2,) + part, low),
        ],
        scratch_shapes=[
            pltpu.VMEM((every, ext, 2 * HD), low),
            pltpu.VMEM((every, ext, 2 * HD), low),
            pltpu.VMEM((every, 2 * HD, ext), low),
            pltpu.VMEM((every, ext, 2 * HD), f32),
            pltpu.VMEM((every, ext, 2 * HD), f32),
            edge, edge, pair, pair, pair, pair, pair,
            pltpu.SemaphoreType.DMA((2, seqs)),
            pltpu.SemaphoreType.DMA((3, 2)),
            pltpu.SemaphoreType.DMA((2, 2)),
            pltpu.SemaphoreType.DMA((2, 2)),
            pltpu.SemaphoreType.DMA((2, 2)),
            pltpu.SemaphoreType.DMA((2, 2)),
        ],
        compiler_params=pltpu.CompilerParams(vmem_limit_bytes=62 * 2**20, collective_id=4, has_side_effects=True),
        name="attend_back",
    )(qkv, halo, augk, q2, out, grad, kept, side)


def finish_kernel(
    g_ref, wt_ref, x_ref, gres_ref, small_ref, sums_ref, out_kept, gvec_ref, gfcb_ref, z_hbm,
    input_grad_ref, fc_total_ref, proj_total_ref, out_total_ref, qkv_total_ref, vec_ref,
    z_all, odd, odd_in, even, mine, first_in, second_in, mt, rows6, vec_out, vec_in, vec_line,
    acc, acc_out, acc_q, left, left_out, left_q, right, right_out, right_q, out_near, out_far, out_mid,
    z_sem, odd_send, odd_recv, near_send, near_recv, far_send, far_recv,
    vec_send, vec_recv, vl_send, vl_recv, line_send, line_recv, out_send, out_recv,
):
    group = small_ref.shape[0]
    me = lax.axis_index("fsdp")
    line = lax.axis_index("seq")
    line_size = 4
    at = [xor(me, k, group) for k in range(group)]
    block = x_ref.shape[0] // 2
    f32, low = jnp.float32, jnp.bfloat16
    width = x_ref.shape[1]
    span = small_ref.shape[2]
    heads = wt_ref.shape[0] // (3 * HD)
    outer = (line == 0) | (line == line_size - 1)
    inner = (line > 0) & (line < line_size - 1)

    def remote(src, dst, send, recv, to):
        return pltpu.make_async_remote_copy(
            src_ref=src, dst_ref=dst, send_sem=send, recv_sem=recv, device_id=to, device_id_type=MESH
        )

    barrier = pltpu.get_barrier_semaphore()
    for peer in at[1:]:
        pl.semaphore_signal(barrier, inc=1, device_id={"fsdp": peer}, device_id_type=MESH)
    others = [lax.rem(line + d, line_size) for d in range(1, line_size)]
    for other in others:
        pl.semaphore_signal(barrier, inc=1, device_id={"seq": other}, device_id_type=MESH)
    pl.semaphore_wait(barrier, group - 1 + line_size - 1)

    cut = sums_ref.shape[1] // 4
    fc_chunks, proj_chunks = [], []
    for i in range(4):
        part = pl.ds(i * cut, cut)
        fc_chunks.append([r.at[0, part] for r in (sums_ref, acc, left, right)] + [fc_total_ref.at[part]])
        there = proj_total_ref.at[pl.ds(i % 2 * cut, cut), pl.ds(i // 2 * sums_ref.shape[2], sums_ref.shape[2])]
        proj_chunks.append([r.at[1, part] for r in (sums_ref, acc, left, right)] + [there])
    cut = acc_q.shape[0] // 3
    qkv_chunks = [
        [r.at[pl.ds(i * cut, cut)] for r in (acc_q, acc_q, left_q, right_q, qkv_total_ref)] for i in range(3)
    ]
    out_chunk = [acc_out, acc_out, left_out, right_out, out_total_ref]
    chunks = fc_chunks + proj_chunks[:1] + qkv_chunks + proj_chunks[1:] + [out_chunk]
    early = 5

    def inwards(c):
        return remote(
            chunks[c][0], chunks[c][2], line_send.at[0, c], line_recv.at[0, c], {"seq": 1 + lax.div(line, line_size - 1)}
        )

    def across(c):
        return remote(
            chunks[c][1], chunks[c][3], line_send.at[1, c], line_recv.at[1, c], {"seq": line_size - 1 - line}
        )

    def outwards(c):
        return remote(
            chunks[c][4], chunks[c][3], line_send.at[2, c], line_recv.at[2, c],
            {"seq": lax.rem((line + line_size - 1) * (line_size - 1), 2 * (line_size - 1))},
        )

    def begin(cs):
        @pl.when(outer)
        def _():
            for c in cs:
                inwards(c).start()

    def collect(c):
        @pl.when(inner)
        def _():
            inwards(c).wait_recv()
            own, acc_c, left_c = chunks[c][:3]
            acc_c[...] = (own[...].astype(f32) + left_c[...].astype(f32)).astype(low)
            across(c).start()

    def settle(c):
        @pl.when(inner)
        def _():
            across(c).wait_recv()
            chunks[c][4][...] = (chunks[c][1][...].astype(f32) + chunks[c][3][...].astype(f32)).astype(low)
            outwards(c).start()

    def receive(c):
        @pl.when(outer)
        def _():
            outwards(c).wait_recv()
            chunks[c][4][...] = chunks[c][3][...]

    def advance(first, last):
        for c in range(first, last):
            collect(c)
            if c >= 1:
                settle(c - 1)
            if c >= 2:
                receive(c - 2)

    begin(range(early))
    load = pltpu.make_async_copy(z_hbm, z_all, z_sem)
    load.start()

    ways = (at[2], at[4])
    out_cut = out_kept.shape[1] // 2
    out_first = ((0, 1, 0), (0, 3, 1), (1, 2, 0), (1, 3, 1))

    def out_near_copy(n):
        h, slot, j = out_first[n]
        return pltpu.make_async_remote_copy(
            src_ref=out_kept.at[slot, pl.ds(h * out_cut, out_cut)], dst_ref=out_near.at[h, j], send_sem=out_send.at[n],
            recv_sem=out_recv.at[n], device_id={"fsdp": ways[h]}, device_id_type=MESH,
        )

    def out_far_copy(h):
        return pltpu.make_async_remote_copy(
            src_ref=out_mid.at[h], dst_ref=out_far.at[h], send_sem=out_send.at[4 + h],
            recv_sem=out_recv.at[4 + h], device_id={"fsdp": ways[1 - h]}, device_id_type=MESH,
        )

    for n in range(4):
        out_near_copy(n).start()

    def product(r, s):
        start = pl.multiple_of(at[r] * block, block)
        return nn(g_ref[s, pl.ds(start, block), :], wt_ref[...])

    def odd_copy(j):
        return remote(odd.at[j], odd_in.at[j], odd_send.at[j], odd_recv.at[j], {"fsdp": at[1]})

    for j in (3, 1, 2, 0):
        for s in range(2):
            odd[j, s] = product(2 * j + 1, s).astype(low)
        odd_copy(j).start()
    advance(0, 1)

    def near_copy(s, i):
        j = 3 if i == 0 else 1 + s
        return remote(even.at[j, s], first_in.at[s, i], near_send.at[s, i], near_recv.at[s, i], {"fsdp": ways[s]})

    def far_copy(s):
        return remote(even.at[2 - s, s], second_in.at[s], far_send.at[s], far_recv.at[s], {"fsdp": ways[1 - s]})

    for j in (3, 1, 2, 0):
        for s in range(2):
            part = product(2 * j, s)
            if s == 0:
                odd_copy(j).wait_recv()
            part += odd_in[j, s].astype(f32)
            if j == 0:
                mine[s] = part
            else:
                even[j, s] = part.astype(low)
                if j == 3:
                    near_copy(s, 0).start()
                elif j == 1 + s:
                    near_copy(s, 1).start()
        if j == 1:
            advance(1, 2)
    advance(2, 3)

    def wide(index):
        return jnp.concatenate([small_ref[f, index : index + 1, :] for f in range(group)], axis=1).astype(f32)

    gain = wide(0)
    load.wait()
    mt[...] = jnp.zeros_like(mt)
    steps = z_all.shape[1] // 512
    ones = jnp.ones((512, 128), low)

    def add_product(i, sums):
        rows = pl.ds(pl.multiple_of(lax.rem(i, steps) * 512, 512), 512)
        g = g_ref[lax.div(i, steps), rows, :]
        mt[...] += tn(g, z_all[lax.div(i, steps), rows, :])
        return sums + tn(g, ones)

    column = lax.fori_loop(0, steps // 2, add_product, jnp.zeros((g_ref.shape[2], 128), f32))
    advance(3, 4)
    column = lax.fori_loop(steps // 2, steps, add_product, column)
    for h in range(2):
        part = slice(h * out_cut, (h + 1) * out_cut)
        out_near_copy(2 * h + 1).wait_recv()
        out_mid[h] = (out_kept[2 - h, part].astype(f32) + out_near[h, 1].astype(f32)).astype(low)
        out_far_copy(h).start()
    advance(4, 5)
    column = lax.fori_loop(steps, 2 * steps, add_product, column)
    acc_q[...] = mt[...].astype(low)
    begin(range(early, len(chunks) - 1))

    def vec_copy(k):
        return remote(vec_out.at[k], vec_in.at[k], vec_send.at[k], vec_recv.at[k], {"fsdp": at[k]})

    for s in range(2):
        near_copy(s, 0).wait_recv()
        even[2 - s, s] = (even[2 - s, s].astype(f32) + first_in[s, 0].astype(f32)).astype(low)
        far_copy(s).start()

    advance(5, 6)
    for h in range(2):
        part = slice(h * out_cut, (h + 1) * out_cut)
        out_near_copy(2 * h).wait_recv()
        out_far_copy(h).wait_recv()
        acc_out[part] = (
            out_kept[0, part].astype(f32) + out_near[h, 0].astype(f32) + out_far[h].astype(f32)
        ).astype(low)
    begin([len(chunks) - 1])

    def line_copy(d):
        return remote(vec_line.at[line], vec_line.at[line], vl_send.at[d], vl_recv.at[d], {"seq": others[d]})

    advance(6, 7)
    gain_grad = offset_grad = jnp.zeros((1, width), f32)
    for s in range(2):
        near_copy(s, 1).wait_recv()
        far_copy(s).wait_recv()
        rows = slice(s * block, (s + 1) * block)
        e = mine[s] + first_in[s, 1].astype(f32) + second_in[s].astype(f32)
        z, rate = standardize(x_ref[rows, :].astype(f32))
        gain_grad += column_sums(e * z)
        offset_grad += column_sums(e)
        input_grad_ref[rows, :] = (gres_ref[rows, :] + norm_grad(e * gain, z, rate)).astype(low)
    rows6[0:1, :] = gain_grad
    rows6[1:2, :] = offset_grad
    rows6[2:6, :] = gvec_ref[0:4, :]
    row = column.T[0:1, :]
    vec_out[...] = jnp.zeros_like(vec_out)
    for k in range(group):
        vec_out[k, 0:6, :] = rows6[0:6, pl.ds(pl.multiple_of(at[k] * span, span), span)]
        for i in range(4):
            vec_out[k, 6 + i : 7 + i, :] = gfcb_ref[STEP_OF[k], :, i * span : (i + 1) * span]
    for h in range(heads):
        base = heads * 2 * HD + h * HD
        vec_out[0, 10 + h : 11 + h, :] = jnp.concatenate(
            [row[:, base : base + HD], row[:, h * 2 * HD + HD : (h + 1) * 2 * HD]], axis=1
        )

    for k in range(1, group):
        vec_copy(k).start()

    advance(7, 9)
    total = vec_out[0]
    for k in range(1, group):
        vec_copy(k).wait_recv()
        total += vec_in[k]
    vec_line[line] = total

    for d in range(line_size - 1):
        line_copy(d).start()

    advance(9, 11)
    for d in range(line_size - 1):
        line_copy(d).wait_recv()
    vec_ref[...] = vec_line[0] + vec_line[1] + vec_line[2] + vec_line[3]
    advance(11, 12)
    settle(11)
    receive(10)
    receive(11)
    for j in range(4):
        odd_copy(j).wait_send()
    for s in range(2):
        near_copy(s, 0).wait_send()
        near_copy(s, 1).wait_send()
        far_copy(s).wait_send()
    for n in range(4):
        out_near_copy(n).wait_send()
    for h in range(2):
        out_far_copy(h).wait_send()
    for k in range(1, group):
        vec_copy(k).wait_send()
    for d in range(line_size - 1):
        line_copy(d).wait_send()

    @pl.when(outer)
    def _():
        for c in range(len(chunks)):
            inwards(c).wait_send()

    @pl.when(inner)
    def _():
        for c in range(len(chunks)):
            across(c).wait_send()
            outwards(c).wait_send()


def finish(g, wt, x, gres, small, sums, out_kept, gvec, gfcb, z_all):
    rows, width = x.shape
    group = small.shape[0]
    half = rows // 2
    span = small.shape[2]
    f32, low = jnp.float32, jnp.bfloat16
    vmem = pl.BlockSpec(memory_space=pltpu.VMEM)
    dma = pltpu.SemaphoreType.DMA
    out_part = out_kept.shape[1:]
    half_out = (out_part[0] // 2, out_part[1])
    buffers = [pltpu.VMEM(sums.shape, low), pltpu.VMEM(out_part, low), pltpu.VMEM(wt.shape, low)]
    return pl.pallas_call(
        finish_kernel,
        in_specs=[vmem] * 9 + [pl.BlockSpec(memory_space=pl.ANY)],
        out_specs=[vmem] * 6,
        out_shape=[
            jax.ShapeDtypeStruct((rows, width), low),
            jax.ShapeDtypeStruct(sums.shape[1:], low),
            jax.ShapeDtypeStruct((sums.shape[2], sums.shape[1]), low),
            jax.ShapeDtypeStruct(out_part, low),
            jax.ShapeDtypeStruct(wt.shape, low),
            jax.ShapeDtypeStruct((16, span), f32),
        ],
        scratch_shapes=[
            pltpu.VMEM(z_all.shape, low),
            pltpu.VMEM((group // 2, 2, half, width), low),
            pltpu.VMEM((group // 2, 2, half, width), low),
            pltpu.VMEM((group // 2, 2, half, width), low),
            pltpu.VMEM((2, half, width), f32),
            pltpu.VMEM((2, 2, half, width), low),
            pltpu.VMEM((2, half, width), low),
            pltpu.VMEM(wt.shape, f32),
            pltpu.VMEM((8, width), f32),
            pltpu.VMEM((group, 16, span), f32),
            pltpu.VMEM((group, 16, span), f32),
            pltpu.VMEM((4, 16, span), f32),
        ]
        + buffers * 3
        + [pltpu.VMEM((2, 2) + half_out, low), pltpu.VMEM((2,) + half_out, low), pltpu.VMEM((2,) + half_out, low)]
        + [dma, dma((4,)), dma((4,)), dma((2, 2)), dma((2, 2)), dma((2,)), dma((2,))]
        + [dma((group,)), dma((group,)), dma((3,)), dma((3,)), dma((3, 12)), dma((3, 12)), dma((6,)), dma((6,))],
        compiler_params=pltpu.CompilerParams(vmem_limit_bytes=62 * 2**20, collective_id=5, has_side_effects=True),
        name="finish",
    )(g, wt, x, gres, small, sums, out_kept, gvec, gfcb, z_all)


def plain_fill_keys(heads, qkv_ref, halo_ref, augk_ref, keys, values):
    halo_rows = halo_ref.shape[1]
    rows = qkv_ref.shape[1]
    ones = jnp.ones((1, HD), jnp.bfloat16)
    for h in range(heads):
        c = h * 2 * HD
        for source, base, size in ((halo_ref, 0, halo_rows), (qkv_ref, halo_rows, rows)):
            pair = source[0, :, c : c + 2 * HD]
            keys[h, base : base + size, :] = jnp.concatenate(
                [pair[:, :HD], augk_ref[0, base : base + size, :]], axis=1
            )
            values[h, base : base + size, :] = jnp.concatenate(
                [pair[:, HD:], jnp.broadcast_to(ones, (size, HD))], axis=1
            )


def plain_attend_kernel(heads, qkv_ref, halo_ref, augk_ref, augq_ref, out_ref, q2_ref, keys, values, values_t):
    step = pl.program_id(1)
    nkeys = keys.shape[1]

    @pl.when(step == 0)
    def _():
        plain_fill_keys(heads, qkv_ref, halo_ref, augk_ref, keys, values)
        for h in range(heads):
            for b in range(nkeys // BLK):
                values_t[h, :, b * BLK : (b + 1) * BLK] = values[h, b * BLK : (b + 1) * BLK, :].T

    mask = edge_mask()
    tiles = WINDOW // BLK + 1
    start = pl.multiple_of(step * BLK, BLK)
    lane = lax.broadcasted_iota(jnp.int32, (BLK, 2 * HD), 1)
    lse_lane = augq_ref.shape[2] + HD - 3
    for h in range(heads):
        qc = heads * 2 * HD + h * HD
        q = jnp.concatenate([qkv_ref[0, pl.ds(start, BLK), qc : qc + HD] * 0.125, augq_ref[0]], axis=1)
        scores = [nt(keys[h, pl.ds(start + b * BLK, BLK), :], q) for b in range(tiles)]
        scores = merge_edges(mask, scores)
        peak = functools.reduce(jnp.maximum, scores)
        peak = jnp.max(peak, axis=0, keepdims=True)
        weights = spread_edges(mask, [jnp.exp(s - peak).astype(jnp.bfloat16) for s in scores])
        total = sum(
            nn(values_t[h, :, pl.ds(pl.multiple_of(start + b * BLK, BLK), BLK)], w) for b, w in enumerate(weights)
        )
        sub = lax.broadcasted_iota(jnp.int32, total.shape, 0)
        total = jnp.where(sub == HD + 1, peak, total).T
        norm = total[:, HD : HD + 1]
        out_ref[0, :, h * HD : (h + 1) * HD] = (total[:, :HD] / norm).astype(out_ref.dtype)
        lse = total[:, HD + 1 : HD + 2] + jnp.log(norm)
        hi, mid, low = split3(-lse)
        q2 = q.astype(jnp.float32)
        q2 = jnp.where(lane == lse_lane, hi, q2)
        q2 = jnp.where(lane == lse_lane + 1, mid, q2)
        q2 = jnp.where(lane == lse_lane + 2, low, q2)
        q2_ref[0, h] = q2.astype(jnp.bfloat16)


def plain_attend(qkv, halo, augk, augq, heads):
    seqs, rows, cols = qkv.shape
    ext = augk.shape[1]
    return pl.pallas_call(
        functools.partial(plain_attend_kernel, heads),
        grid=(seqs, rows // BLK),
        in_specs=[
            pl.BlockSpec((1, rows, cols), lambda s, i: (s, 0, 0)),
            pl.BlockSpec((1, WINDOW, heads * 2 * HD), lambda s, i: (s, 0, 0)),
            pl.BlockSpec((1, ext, HD), lambda s, i: (s, 0, 0)),
            pl.BlockSpec((1, BLK, HD), lambda s, i: (s, i, 0)),
        ],
        out_specs=[
            pl.BlockSpec((1, BLK, heads * HD), lambda s, i: (s, i, 0)),
            pl.BlockSpec((1, heads, BLK, 2 * HD), lambda s, i: (s, 0, i, 0)),
        ],
        out_shape=[
            jax.ShapeDtypeStruct((seqs, rows, heads * HD), jnp.bfloat16),
            jax.ShapeDtypeStruct((seqs, heads, rows, 2 * HD), jnp.bfloat16),
        ],
        scratch_shapes=[
            pltpu.VMEM((heads, ext, 2 * HD), jnp.bfloat16),
            pltpu.VMEM((heads, ext, 2 * HD), jnp.bfloat16),
            pltpu.VMEM((heads, 2 * HD, ext), jnp.bfloat16),
        ],
        compiler_params=pltpu.CompilerParams(vmem_limit_bytes=48 * 2**20),
        name="plain_attend",
    )(qkv, halo, augk, augq)


def plain_attend_back_kernel(
    heads, qkv_ref, halo_ref, augk_ref, q2_ref, out_ref, grad_ref, dq_ref, dkv_ref, dhalo_ref,
    keys, values, keys_t, dkeys, dvalues,
):
    step = pl.program_id(1)
    nkeys = keys.shape[1]

    @pl.when(step == 0)
    def _():
        plain_fill_keys(heads, qkv_ref, halo_ref, augk_ref, keys, values)
        for h in range(heads):
            for b in range(nkeys // BLK):
                keys_t[h, :, b * BLK : (b + 1) * BLK] = keys[h, b * BLK : (b + 1) * BLK, :].T
        dkeys[...] = jnp.zeros_like(dkeys)
        dvalues[...] = jnp.zeros_like(dvalues)

    mask = edge_mask()
    tiles = WINDOW // BLK + 1
    start = pl.multiple_of(step * BLK, BLK)
    lane = lax.broadcasted_iota(jnp.int32, (BLK, 2 * HD), 1)
    for h in range(heads):
        q = q2_ref[0, h]
        g = grad_ref[0, :, h * HD : (h + 1) * HD]
        g32 = g.astype(jnp.float32)
        centre = jnp.sum(g32 * out_ref[0, :, h * HD : (h + 1) * HD].astype(jnp.float32), axis=1, keepdims=True)
        hi, mid, low = split3(-centre)
        g2 = jnp.concatenate([g32, jnp.zeros((BLK, HD), jnp.float32)], axis=1)
        g2 = jnp.where(lane == HD, hi, g2)
        g2 = jnp.where(lane == HD + 1, mid, g2)
        g2 = jnp.where(lane == HD + 2, low, g2).astype(jnp.bfloat16)
        spans = [pl.ds(pl.multiple_of(start + b * BLK, BLK), BLK) for b in range(tiles)]
        scores = merge_edges(mask, [nt(keys[h, s, :], q) for s in spans])
        wgrads = merge_edges(mask, [nt(values[h, s, :], g2) for s in spans])
        weights = [jnp.exp(s) for s in scores]
        sgrads = spread_edges(mask, [(w * d).astype(jnp.bfloat16) for w, d in zip(weights, wgrads)])
        weights = spread_edges(mask, [w.astype(jnp.bfloat16) for w in weights])
        for s, w, d in zip(spans, weights, sgrads):
            dvalues[h, s, :] += nn(w, g2)
            dkeys[h, s, :] += nn(d, q)
        dq = sum(nn(keys_t[h, :, s], d) for s, d in zip(spans, sgrads))
        dq_ref[0, :, h * HD : (h + 1) * HD] = (dq.T[:, :HD] * 0.125).astype(dq_ref.dtype)

    @pl.when(step == pl.num_programs(1) - 1)
    def _():
        for h in range(heads):
            c = h * 2 * HD
            dhalo_ref[0, :, c : c + 2 * HD] = jnp.concatenate(
                [dkeys[h, :WINDOW, :HD], dvalues[h, :WINDOW, :HD]], axis=1
            ).astype(dhalo_ref.dtype)
            dkv_ref[0, :, c : c + 2 * HD] = jnp.concatenate(
                [dkeys[h, WINDOW:, :HD], dvalues[h, WINDOW:, :HD]], axis=1
            ).astype(dkv_ref.dtype)


def plain_attend_back(qkv, halo, augk, q2, out, grad, heads):
    seqs, rows, cols = qkv.shape
    ext = augk.shape[1]
    return pl.pallas_call(
        functools.partial(plain_attend_back_kernel, heads),
        grid=(seqs, rows // BLK),
        in_specs=[
            pl.BlockSpec((1, rows, cols), lambda s, i: (s, 0, 0)),
            pl.BlockSpec((1, WINDOW, heads * 2 * HD), lambda s, i: (s, 0, 0)),
            pl.BlockSpec((1, ext, HD), lambda s, i: (s, 0, 0)),
            pl.BlockSpec((1, heads, BLK, 2 * HD), lambda s, i: (s, 0, i, 0)),
            pl.BlockSpec((1, BLK, heads * HD), lambda s, i: (s, i, 0)),
            pl.BlockSpec((1, BLK, heads * HD), lambda s, i: (s, i, 0)),
        ],
        out_specs=[
            pl.BlockSpec((1, BLK, heads * HD), lambda s, i: (s, i, 0)),
            pl.BlockSpec((1, rows, heads * 2 * HD), lambda s, i: (s, 0, 0)),
            pl.BlockSpec((1, WINDOW, heads * 2 * HD), lambda s, i: (s, 0, 0)),
        ],
        out_shape=[
            jax.ShapeDtypeStruct((seqs, rows, heads * HD), jnp.bfloat16),
            jax.ShapeDtypeStruct((seqs, rows, heads * 2 * HD), jnp.float32),
            jax.ShapeDtypeStruct((seqs, WINDOW, heads * 2 * HD), jnp.bfloat16),
        ],
        scratch_shapes=[
            pltpu.VMEM((heads, ext, 2 * HD), jnp.bfloat16),
            pltpu.VMEM((heads, ext, 2 * HD), jnp.bfloat16),
            pltpu.VMEM((heads, 2 * HD, ext), jnp.bfloat16),
            pltpu.VMEM((heads, ext, 2 * HD), jnp.float32),
            pltpu.VMEM((heads, ext, 2 * HD), jnp.float32),
        ],
        compiler_params=pltpu.CompilerParams(vmem_limit_bytes=56 * 2**20),
        name="plain_attend_back",
    )(qkv, halo, augk, q2, out, grad)


def from_behind(block, axis, distance):
    devices = range(lax.axis_size(axis))
    route = [(i - distance, i) for i in devices if i - distance in devices]
    return lax.ppermute(block, axis, route)


def pack_columns(array, heads):
    parts = array.reshape(array.shape[:-1] + (heads, 3 * HD))
    lead = array.shape[:-1]
    return jnp.concatenate(
        [parts[..., HD:].reshape(lead + (-1,)), parts[..., :HD].reshape(lead + (-1,))], axis=-1
    )


def unpack_columns(array, heads):
    lead = array.shape[:-1]
    pairs = array[..., : heads * 2 * HD].reshape(lead + (heads, 2 * HD))
    queries = array[..., heads * 2 * HD :].reshape(lead + (heads, HD))
    return jnp.concatenate([queries, pairs], axis=-1).reshape(lead + (-1,))


def dot(subscripts, a, b):
    return jnp.einsum(subscripts, a, b, preferred_element_type=jnp.float32)


def general_body(
    inputs, cotangent, segment_ids, norm1_gain, norm1_bias, qkv_weight, qv_bias, out_weight, out_bias,
    norm2_gain, norm2_bias, fc_weight, fc_bias, proj_weight, proj_bias,
):
    group = lax.axis_size("fsdp")
    seqs, local_rows, width = inputs.shape
    part_rows = local_rows * group
    heads = qkv_weight.shape[1] // (3 * HD)
    docs = segment_ids.shape[1] // (2 * WINDOW)
    seq_index = lax.axis_index("seq")
    shard = norm1_gain.shape[0]

    small = jnp.concatenate([norm1_gain, norm1_bias, out_bias, norm2_gain, norm2_bias, proj_bias, fc_bias])
    small = lax.all_gather(small, "fsdp")
    gain1, offset1, out_off, gain2, offset2, proj_off = (
        small[:, i * shard : (i + 1) * shard].reshape(-1).astype(jnp.float32) for i in range(6)
    )
    fc_off = small[:, 6 * shard :].reshape(-1).astype(jnp.float32)
    out_all = lax.all_gather(out_weight, "fsdp", axis=0, tiled=True)
    fc_all = lax.all_gather(fc_weight, "fsdp")
    proj_all = lax.all_gather(proj_weight, "fsdp")

    padded_ids = jnp.concatenate([jnp.full((seqs, WINDOW), -1, jnp.int32), segment_ids], axis=1)
    segment_ext = lax.dynamic_slice_in_dim(padded_ids, seq_index * part_rows, WINDOW + part_rows, 1)
    augk, augq = mask_features(segment_ext, docs)

    x = inputs.astype(jnp.float32)
    z1, rate1 = standardize(x)
    normed1 = (z1 * gain1 + offset1).astype(jnp.bfloat16)
    normed1 = lax.all_gather(normed1, "fsdp", axis=1, tiled=True)
    packed_weight = pack_columns(qkv_weight, heads)
    head_bias = qv_bias.astype(jnp.float32)
    head_bias = jnp.concatenate(
        [head_bias[:, :HD], jnp.zeros((heads, HD), jnp.float32), head_bias[:, HD:]], axis=1
    ).reshape(-1)
    packed_bias = pack_columns(head_bias, heads)
    qkv = (dot("sre,ef->srf", normed1, packed_weight) + packed_bias).astype(jnp.bfloat16)
    halo = from_behind(qkv[:, part_rows - WINDOW :, : heads * 2 * HD], "seq", 1)
    head_out, q2 = plain_attend(qkv, halo, augk, augq, heads)
    merged = lax.all_to_all(head_out, "fsdp", split_axis=1, concat_axis=2, tiled=True)
    resid = x + dot("sre,ef->srf", merged, out_all) + out_off
    z2, rate2 = standardize(resid)
    normed2 = (z2 * gain2 + offset2).astype(jnp.bfloat16)
    fc_offset = fc_off.reshape(group, -1)
    hidden = dot("sre,gef->gsrf", normed2, fc_all) + fc_offset[:, None, None]
    active, gelu_back = jax.vjp(lambda v: jax.nn.gelu(v, approximate=True), hidden)
    active = active.astype(jnp.bfloat16)
    layer_output = (resid + dot("gsrf,gfd->srd", active, proj_all) + proj_off).astype(jnp.bfloat16)

    cot32 = cotangent.astype(jnp.float32)
    proj_bias_part = jnp.sum(cot32, axis=(0, 1))
    proj_weight_part = dot("gsrf,srd->gfd", active, cotangent)
    g_hidden = gelu_back(dot("srd,gfd->gsrf", cotangent, proj_all))[0].astype(jnp.bfloat16)
    fc_bias_part = jnp.sum(g_hidden, axis=(1, 2), dtype=jnp.float32).reshape(-1)
    fc_weight_part = dot("sre,gsrf->gef", normed2, g_hidden)
    g_norm2 = dot("gsrf,gef->sre", g_hidden, fc_all)
    gain2_part = jnp.sum(g_norm2 * z2, axis=(0, 1))
    offset2_part = jnp.sum(g_norm2, axis=(0, 1))
    g_resid = cot32 + norm_grad(g_norm2 * gain2, z2, rate2)
    g_attn = g_resid.astype(jnp.bfloat16)
    out_bias_part = jnp.sum(g_attn, axis=(0, 1), dtype=jnp.float32)
    out_weight_part = dot("sre,srd->ed", merged, g_attn)
    g_merged = dot("srd,ed->sre", g_attn, out_all).astype(jnp.bfloat16)
    g_heads = lax.all_to_all(g_merged, "fsdp", split_axis=2, concat_axis=1, tiled=True)

    low = jnp.bfloat16
    fc_grad = lax.psum_scatter(fc_weight_part.astype(low), "fsdp")
    proj_grad = lax.psum_scatter(proj_weight_part.astype(low), "fsdp")
    out_grad = lax.psum_scatter(out_weight_part.astype(low), "fsdp", scatter_dimension=0, tiled=True)
    fc_grad, proj_grad, out_grad = lax.psum((fc_grad, proj_grad, out_grad), "seq")

    dq, dkv, dhalo = plain_attend_back(qkv, halo, augk, q2, head_out, g_heads, heads)
    edge = from_behind(dhalo, "seq", -1)
    edge = jnp.pad(edge.astype(jnp.float32), ((0, 0), (part_rows - WINDOW, 0), (0, 0)))
    g_qkv = jnp.concatenate([(dkv + edge).astype(jnp.bfloat16), dq], axis=-1)
    qkv_grad = dot("sre,srf->ef", normed1, g_qkv)
    qkv_colsum = jnp.sum(g_qkv, axis=(0, 1), dtype=jnp.float32)
    g_norm1 = dot("srf,ef->sre", g_qkv, packed_weight).astype(jnp.bfloat16)
    g_norm1 = lax.psum_scatter(g_norm1, "fsdp", scatter_dimension=1, tiled=True).astype(jnp.float32)
    gain1_part = jnp.sum(g_norm1 * z1, axis=(0, 1))
    offset1_part = jnp.sum(g_norm1, axis=(0, 1))
    input_grad = (g_resid + norm_grad(g_norm1 * gain1, z1, rate1)).astype(jnp.bfloat16)

    qkv_grad = lax.psum(qkv_grad.astype(low), "seq").astype(jnp.float32)
    qkv_grad = unpack_columns(qkv_grad, heads)
    col = unpack_columns(qkv_colsum, heads).reshape(heads, 3 * HD)
    col = lax.psum(jnp.concatenate([col[:, :HD], col[:, 2 * HD :]], axis=1), "seq")
    vectors = jnp.concatenate(
        [
            v.reshape(group, -1)
            for v in (gain1_part, offset1_part, out_bias_part, gain2_part, offset2_part, proj_bias_part, fc_bias_part)
        ],
        axis=1,
    )
    vectors = lax.psum_scatter(vectors, "fsdp")
    vectors = lax.psum(vectors, "seq")
    parts = [vectors[i * shard : (i + 1) * shard] for i in range(6)] + [vectors[6 * shard :]]
    f32 = jnp.float32
    return (
        layer_output, input_grad, parts[0], parts[1], qkv_grad, col, out_grad.astype(f32), parts[2], parts[3],
        parts[4], fc_grad.astype(f32), parts[6], proj_grad.astype(f32), parts[5],
    )


def cube_body(
    inputs, cotangent, segment_ids, norm1_gain, norm1_bias, qkv_weight, qv_bias, out_weight, out_bias,
    norm2_gain, norm2_bias, fc_weight, fc_bias, proj_weight, proj_bias,
):
    group = lax.axis_size("fsdp")
    seqs, local_rows, width = inputs.shape
    part_rows = local_rows * group
    heads = qkv_weight.shape[1] // (3 * HD)
    docs = segment_ids.shape[1] // (2 * WINDOW)
    seq_index = lax.axis_index("seq")
    me = lax.axis_index("fsdp")
    shard = norm1_gain.shape[0]
    f32, low = jnp.float32, jnp.bfloat16

    smalls = [norm1_gain, norm1_bias, out_bias, norm2_gain, norm2_bias, proj_bias, fc_bias]
    smalls = [v.reshape(-1, shard) for v in smalls]
    padded_ids = jnp.concatenate([jnp.full((seqs, WINDOW), -1, jnp.int32), segment_ids], axis=1)
    segment_ext = lax.dynamic_slice_in_dim(padded_ids, seq_index * part_rows, WINDOW + part_rows, 1)
    augk, augq = mask_features(segment_ext, docs)
    packed_weight = pack_columns(qkv_weight, heads)
    head_bias = qv_bias.astype(f32)
    head_bias = jnp.concatenate(
        [head_bias[:, :HD], jnp.zeros((heads, HD), f32), head_bias[:, HD:]], axis=1
    ).reshape(-1)
    packed_bias = pack_columns(head_bias, heads)

    x = inputs.reshape(seqs * local_rows, width)
    cot = cotangent.reshape(seqs * local_rows, width)
    all_small, z1, qkv = gather_project(x, smalls, packed_weight, packed_bias[None], group)
    head_out, q2, halo, merged, out_all, fc_near, proj_near = attend(
        qkv, augk, augq, out_weight, fc_weight, proj_weight, heads, group
    )
    full = lambda i: all_small[:, i].reshape(-1).astype(f32)
    vectors = jnp.stack([full(2), full(3), full(4), full(5)] + [jnp.zeros((width,), f32)] * 4)
    slots = jnp.stack([xor(me, r, group) for r in SLOT_AT])
    fc_off = jnp.take(all_small[:, 6:10].reshape(group, -1), slots, axis=0).astype(f32)[:, None]
    layer_output, g_resid, g_heads, kept, side, out_kept, gvec, gfcb = feed_forward(
        x, cot, merged.reshape(x.shape), out_all.reshape(width, width), fc_near, proj_near, fc_weight, proj_weight, fc_off, vectors
    )
    g_qkv, sums = attend_back(qkv, halo, augk, q2, head_out, g_heads, kept, side, heads, group)
    input_grad, fc_grad, proj_grad, out_grad, qkv_grad, vecs = finish(
        g_qkv, packed_weight.T, x, g_resid, all_small, sums, out_kept, gvec, gfcb, z1
    )
    qkv_grad = unpack_columns(qkv_grad.T.astype(f32), heads)
    return (
        layer_output.reshape(inputs.shape), input_grad.reshape(inputs.shape), vecs[0], vecs[1], qkv_grad,
        vecs[10 : 10 + heads], out_grad.astype(f32), vecs[2], vecs[3], vecs[4], fc_grad.astype(f32), vecs[6:10].reshape(-1),
        proj_grad.astype(f32), vecs[5],
    )


def solution(mesh):
    tokens = P(None, ("seq", "fsdp"), None)
    rows, cols, vec = P("fsdp", None), P(None, "fsdp"), P("fsdp")
    return jax.shard_map(
        cube_body if mesh.shape["fsdp"] == 8 and mesh.shape["seq"] == 4 else general_body,
        mesh=mesh,
        in_specs=(tokens, tokens, P(), vec, vec, cols, rows, rows, vec, vec, vec, cols, vec, rows, vec),
        out_specs=(tokens, tokens, vec, vec, cols, rows, rows, vec, vec, vec, cols, vec, rows, vec),
        check_vma=False,
    )
```

profile of v0, /device:TPU:0, one launch (start us, length us, event | category | flops | bytes accessed | tf_op | source)
XLA Modules:
  0.0 372.9 jit_solution(18324224864347541726)
XLA Ops:
  1.3 0.8 fusion.8
  3.0 1.4 copy.33
  4.5 1.0 fusion.7
  5.8 0.9 copy.35
  6.7 1.1 fusion.2
  7.9 2.2 maximum_maximum_fusion.augk_ref
  10.1 1.1 fusion
  11.4 1.3 maximum_maximum_fusion.1.augq_ref
  12.8 46.7 %gather_project.1 = (bf16[8,16,128]{2,1,0:T(8,128)(2,1)S(1)}, bf16[2,2048,1024]{2,1,0:T(8,128)(2,1)}, bf16[2,2048,384]{2,1,0:T(8,128)(2,1)S(1)}) custom-call(bf16[512,1024]{1,0:T(8,128)(2,1)S(1)} %bitcast.80, bf16[1,128]{1,0:T(2,128)(2,1)S(1)} %bitcast.82, bf16[1,128]{1,0:T(2,128)(2,1)S(1)} %bitcast.83, bf16[1,128]{1,0:T(2,128)(2,1)S(1)} %bitcast.84, ...), custom_call_target="tpu_custom_call" | custom-call | tf_op jit(solution)/shard_map/gather_project/pallas_call | solution.py:494
  59.5 1.8 copy-done
  63.3 63.1 %attend.1 = (bf16[2,2048,128]{2,1,0:T(8,128)(2,1)}, bf16[2,2,2048,128]{3,2,1,0:T(8,128)(2,1)}, bf16[2,1024,256]{2,1,0:T(8,128)(2,1)}, bf16[2,256,1024]{2,1,0:T(8...) custom-call(bf16[2,2048,384]{2,1,0:T(8,128)(2,1)} %copy-done, ...), custom_call_target="tpu_custom_call" | custom-call | tf_op jit(solution)/shard_map/attend/pallas_call | solution.py:332
  126.4 68.4 %feed_forward.1 = (bf16[512,1024]{1,0:T(8,128)(2,1)}, f32[512,1024]{1,0:T(8,128)}, bf16[2,2048,128]{2,1,0:T(8,128)(2,1)}, bf16[4,2,1024,512]{3,2,1,0:T(8,128)(2,...) custom-call(bf16[512,1024]{1,0:T(8,128)(2,1)} %bitcast.78, ...), custom_call_target="tpu_custom_call" | custom-call | tf_op jit(solution)/shard_map/feed_forward/pallas_call | solution.py:744
  194.8 65.4 %attend_back.1 = (bf16[2,2048,384]{2,1,0:T(8,128)(2,1)}, bf16[2,1024,512]{2,1,0:T(8,128)(2,1)}) custom-call(bf16[2,2048,384]{2,1,0:T(8,128)(2,1)} %copy-done, bf16[2,1024,256]{2,1,0:T(8,128)(2,1)} %get-tuple-element.47.halo_ref, bf16[2,3072,64]{2,1,0:T(8,128)(2,1)} %maximum_maximum_fusion.augk_ref, bf16[2,2,2048,128]{3,2,1,0:T(8,128)(2,1)} %get-tuple-element.48.q2_ref, ...), custom_call_target="tpu_custom_call" | custom-call | tf_op jit(solution)/shard_map/attend_back/pallas_call | solution.py:985
  260.2 98.4 %finish.1 = (bf16[512,1024]{1,0:T(8,128)(2,1)}, bf16[1024,512]{1,0:T(8,128)(2,1)}, bf16[512,1024]{1,0:T(8,128)(2,1)}, bf16[128,1024]{1,0:T(8,128)(2,1)}, bf16[384,1024]{1,0:T(8,128)(2,1)}, /*index=5*/f32[16,128]{1,0:T(8,128)}) custom-call(bf16[2,2048,384]{2,1,0:T(8,128)(2,1)} %get-tuple-element.53.g_ref, bf16[384,1024]{1,0:T(8,128)(2,1)} %get-tuple-element.82.wt_ref, ...), custom_call_target="tpu_custom_call" | custom-call | tf_op jit(solution)/shard_map/finish/pallas_call | solution.py:1315
  358.6 1.2 slice.74
  359.8 1.3 slice_bitcast_fusion.1
  361.1 1.4 slice_bitcast_fusion.2
  362.5 1.8 convert_element_type.100
  364.3 1.3 convert_bitcast_fusion
  365.9 1.6 copy.37
  367.5 1.6 convert_element_type.101
  369.1 1.6 convert_element_type.102
  370.7 1.0 copy.46
  371.7 1.0 copy.47
  (58 shorter events, 4.3 us)
Async XLA Ops:
  11.2 1.6 copy-start.1
  11.2 1.5 copy-start.3
  11.2 1.5 copy-start.4
  11.2 1.5 copy-start.5
  11.2 1.5 copy-start.6
  11.3 1.5 copy-start.7
  11.3 1.5 copy-start.8
  11.3 1.5 copy-start.9
  59.5 1.8 copy-start
  61.3 65.1 %copy-start.2 = (bf16[8,16,128]{2,1,0:T(8,128)(2,1)}, bf16[8,16,128]{2,1,0:T(8,128)(2,1)S(1)}, u32[]{:S(2)}) copy-start(bf16[8,16,128]{2,1,0:T(8,128)(2,1)S(1)} %get-tuple-element.45.small_ref) | copy-start | bytes 98308
  365.9 1.6 copy-start.11
  367.5 1.6 copy-start.10
  369.1 1.6 copy-start.12
  369.1 2.5 copy-start.13
where the time goes:
time: 377 us; the launch traced here: 373 us
  Pallas kernels  342 us (91%)
  local copies, waits for them, and re-layouts  14.9 us (4%)
  other arithmetic  14.8 us (4%)
    pallas_call x1, Pallas kernels, finish(): pl.pallas_call(finish_kernel, in_specs=[vmem] * 9 + [pl.BlockSpec(memory_...  98.4 us
    pallas_call x1, Pallas kernels, feed_forward(): pl.pallas_call(functools.partial(feed_forward_kernel, group), grid=(group...  68.4 us
    pallas_call x1, Pallas kernels, attend_back(): pl.pallas_call(functools.partial(attend_back_kernel, heads, group), grid=...  65.4 us
    pallas_call x1, Pallas kernels, attend(): pl.pallas_call(functools.partial(attend_kernel, heads, group), grid=(seqs...  63.1 us
    pallas_call x1, Pallas kernels, gather_project(): pl.pallas_call(gather_project_kernel, in_specs=[vmem] * 10, out_specs=[vm...  46.7 us

commit v1 on v0

--- a/solution.py
+++ b/solution.py
@@ -86,7 +86,7 @@
 
 
 def attend_kernel(
-    heads, group, qkv_ref, augk_ref, augq_ref, out_w, fc_w, proj_w,
+    heads, group, docs, qkv_ref, ids_ref, out_w, fc_w, proj_w,
     out_ref, q2_ref, halo_ref, merged_ref, out_all, fc_all, proj_all,
     keys, values, values_t, sent, behind, own_sems, send_sems, recv_sems, halo_sems, w_own, w_send, w_recv,
 ):
@@ -184,7 +184,7 @@
         w_copy(2, 1).start()
         w_keep(0).start()
         for s in range(seqs):
-            fill_keys(s, heads, qkv_ref, augk_ref, WINDOW, keys, values, values_t, None)
+            fill_keys(s, heads, qkv_ref, ids_ref, docs, WINDOW, keys, values, values_t, None)
 
     @pl.when(step == group)
     def _():
@@ -198,21 +198,20 @@
 
         halo_ref[...] = behind[...]
         for s in range(seqs):
-            fill_keys(s, heads, behind, augk_ref, 0, keys, values, values_t, None)
+            fill_keys(s, heads, behind, ids_ref, docs, 0, keys, values, values_t, None)
 
     mask = edge_mask()
     tiles = WINDOW // BLK + 1
     start = pl.multiple_of(place * BLK, BLK)
     lane = lax.broadcasted_iota(jnp.int32, (BLK, 2 * HD), 1)
-    lse_lane = augq_ref.shape[2] + HD - 3
+    lse_lane = 2 * HD - 3
     slot_k = xor(me, place, group)
     spans = [pl.ds(pl.multiple_of(start + b * BLK, BLK), BLK) for b in range(tiles)]
+    q_marks = query_marks(ids_ref[seq, pl.ds(start + WINDOW, BLK), :], docs)
     for h in range(heads):
         sh = seq * heads + h
         qc = heads * 2 * HD + h * HD
-        q = jnp.concatenate(
-            [qkv_ref[seq, pl.ds(start, BLK), qc : qc + HD] * 0.125, augq_ref[seq, pl.ds(start, BLK), :]], axis=1
-        )
+        q = jnp.concatenate([qkv_ref[seq, pl.ds(start, BLK), qc : qc + HD] * 0.125, q_marks], axis=1)
         scores = merge_edges(mask, [nt(keys[sh, s, :], q) for s in spans])
         peak = functools.reduce(jnp.maximum, scores)
         peak = jnp.max(peak, axis=0, keepdims=True)
@@ -302,16 +301,29 @@
             halo_copy().wait_send()
 
 
-def fill_keys(s, heads, source, augk_ref, base, keys, values, values_t, keys_t):
+def key_marks(ids, docs):
+    lane = lax.broadcasted_iota(jnp.int32, (ids.shape[0], HD), 1)
+    ids = jnp.broadcast_to(ids, lane.shape)
+    hidden = (lane == ids) | ((lane == docs) & (ids < 0))
+    return jnp.where(hidden, -1.0, jnp.where(lane >= HD - 3, 1.0, 0.0)).astype(jnp.bfloat16)
+
+
+def query_marks(ids, docs):
+    lane = lax.broadcasted_iota(jnp.int32, (ids.shape[0], HD), 1)
+    ids = jnp.broadcast_to(ids, lane.shape)
+    return jnp.where((lane <= docs) & (lane != ids), PENALTY, 0.0).astype(jnp.bfloat16)
+
+
+def fill_keys(s, heads, source, ids_ref, docs, base, keys, values, values_t, keys_t):
     size = BLK
     ones = jnp.ones((size, HD), jnp.bfloat16)
-    first = source.shape[1] - WINDOW if base == 0 else 0
-    for h in range(heads):
-        c = h * 2 * HD
-        for i in range(source.shape[1] // size):
+    for i in range(source.shape[1] // size):
+        span = slice(base + i * size, base + (i + 1) * size)
+        marks = key_marks(ids_ref[s, span, :], docs)
+        for h in range(heads):
+            c = h * 2 * HD
             pair = source[s, i * size : (i + 1) * size, c : c + 2 * HD]
-            span = slice(base + i * size, base + (i + 1) * size)
-            k = jnp.concatenate([pair[:, :HD], augk_ref[s, span, :]], axis=1)
+            k = jnp.concatenate([pair[:, :HD], marks], axis=1)
             v = jnp.concatenate([pair[:, HD:], ones], axis=1)
             keys[s * heads + h, span, :] = k
             values[s * heads + h, span, :] = v
@@ -321,18 +333,18 @@
                 keys_t[s * heads + h, :, span] = k.T
 
 
-def attend(qkv, augk, augq, out_w, fc_w, proj_w, heads, group):
+def attend(qkv, ids, docs, out_w, fc_w, proj_w, heads, group):
     seqs, rows, cols = qkv.shape
-    ext = augk.shape[1]
+    ext = ids.shape[1]
     assert rows // BLK == group
     low = jnp.bfloat16
     vmem = pl.BlockSpec(memory_space=pltpu.VMEM)
     hbm = pl.BlockSpec(memory_space=pl.ANY)
     every = seqs * heads
     return pl.pallas_call(
-        functools.partial(attend_kernel, heads, group),
+        functools.partial(attend_kernel, heads, group, docs),
         grid=(seqs * rows // BLK,),
-        in_specs=[vmem] * 3 + [hbm] * 3,
+        in_specs=[vmem] * 2 + [hbm] * 3,
         out_specs=[vmem] * 3 + [hbm] * 4,
         out_shape=[
             jax.ShapeDtypeStruct((seqs, rows, heads * HD), low),
@@ -357,28 +369,17 @@
         ],
         compiler_params=pltpu.CompilerParams(vmem_limit_bytes=56 * 2**20, collective_id=1, has_side_effects=True),
         name="attend",
-    )(qkv, augk, augq, out_w, fc_w, proj_w)
+    )(qkv, ids, out_w, fc_w, proj_w)
 
 
 def mask_features(segment_ext, docs):
-    doc = jnp.arange(docs, dtype=jnp.int32)
-    hot = (segment_ext[..., None] == doc).astype(jnp.bfloat16)
-    rows = segment_ext.shape[1]
-    outside = (segment_ext < 0).astype(jnp.bfloat16)[..., None]
-    pad = HD - docs - 4
-    one = jnp.ones(segment_ext.shape + (3,), jnp.bfloat16)
-    zero = jnp.zeros(segment_ext.shape + (pad,), jnp.bfloat16)
-    keys = jnp.concatenate([-hot, -outside, zero, one], axis=-1)
-    own = hot[:, WINDOW:]
-    queries = jnp.concatenate(
-        [
-            (1 - own) * jnp.bfloat16(PENALTY),
-            jnp.full(own.shape[:2] + (1,), PENALTY, jnp.bfloat16),
-            jnp.zeros(own.shape[:2] + (pad + 3,), jnp.bfloat16),
-        ],
-        axis=-1,
-    )
-    return keys, queries
+    low = jnp.bfloat16
+    lane = lax.broadcasted_iota(jnp.int32, segment_ext.shape + (HD,), 2)
+    ids = segment_ext[..., None]
+    hidden = (lane == ids) | ((lane == docs) & (ids < 0))
+    keys = jnp.where(hidden, -1.0, jnp.where(lane >= HD - 3, 1.0, 0.0)).astype(low)
+    queries = jnp.where((lane <= docs) & (lane != ids), PENALTY, 0.0).astype(low)
+    return keys, queries[:, WINDOW:]
 
 
 def gather_project_kernel(
@@ -435,7 +436,10 @@
     def project(k, s):
         keep(k, s).start()
         start = pl.multiple_of(at[k] * rows, rows)
-        qkv_ref[s, pl.ds(start, rows), :] = (nn(pieces[at[k], s], w_ref[...]) + b_ref[...]).astype(low)
+        made = (nn(pieces[at[k], s], w_ref[...]) + bias).astype(low)
+        head = [made[:, h * 3 * HD : (h + 1) * 3 * HD] for h in range(heads)]
+        made = jnp.concatenate([h[:, HD:] for h in head] + [h[:, :HD] for h in head], axis=1)
+        qkv_ref[s, pl.ds(start, rows), :] = made
 
     for s in range(2):
         z1[s * rows : (s + 1) * rows, :] = standardize(x_ref[s * rows : (s + 1) * rows, :].astype(f32))[0]
@@ -449,6 +453,10 @@
         move(4, s).start()
         move(1, s).start()
     all_small_ref[...] = smalls[...]
+    heads = b_ref.shape[0]
+    none = jnp.zeros((1, HD), f32)
+    bias = [p for h in range(heads) for p in (b_ref[h : h + 1, :HD].astype(f32), none, b_ref[h : h + 1, HD:].astype(f32))]
+    bias = jnp.concatenate(bias, axis=1)
     for s in range(2):
         project(0, s)
     for s in range(2):
@@ -532,9 +540,9 @@
 
 
 def feed_forward_kernel(
-    group, x_ref, cot_ref, merged_ref, out_ref, fc_near, proj_near, fc_own, proj_own, fcb_ref, vec_ref,
+    group, x_ref, cot_ref, merged_ref, out_ref, fc_near, proj_near, fc_own, proj_own, small_ref,
     layer_ref, gres_ref, gheads_ref, keep_ref, side_ref, gout_ref, gvec_ref, gfcb_ref,
-    resid, z2, rate, normed, total, gnormed, fc_w, proj_w, given, taken, gmerged, gout_given, gout_taken,
+    resid, z2, rate, vec_ref, normed, total, gnormed, fc_w, proj_w, given, taken, gmerged, gout_given, gout_taken,
     load_sems, far_send, far_recv, pair_send, pair_recv, side_send, side_recv, keep_sems, head_send, head_recv,
     own_sem, gout_sems,
 ):
@@ -608,6 +616,10 @@
         for a in range(2):
             far_copy(a, 0).start()
             far_copy(a, 1).start()
+        for i in range(4):
+            vec_ref[i : i + 1, :] = jnp.concatenate(
+                [small_ref[f, 2 + i : 3 + i, :] for f in range(group)], axis=1
+            ).astype(f32)
         acc = x_ref[...].astype(f32) + vec_ref[0:1, :] + nn(merged_ref[...], out_ref[...])
         resid[...] = acc
         z, r = standardize(acc)
@@ -651,7 +663,9 @@
 
     here = jnp.where(step < NEAR, lax.rem(step, 2), step - NEAR + 2)
     fresh = jnp.where(odd == 0, lax.rem(j, 2), 2)
-    hidden = nn(normed[...], fc_w[here]) + fcb_ref[0]
+    owner = sum(jnp.where(step == i, at[SLOT_AT[i]], 0) for i in range(group))
+    fc_bias = jnp.concatenate([small_ref[owner, 6 + i : 7 + i, :] for i in range(4)], axis=1).astype(f32)
+    hidden = nn(normed[...], fc_w[here]) + fc_bias
     gactive = nt(cot_ref[...], proj_w[here])
     active, slope = gelu_both(hidden)
     active = active.astype(low)
@@ -734,9 +748,9 @@
             keep_copy(i).wait()
 
 
-def feed_forward(x, cot, merged, out_all, fc_near, proj_near, fc_own, proj_own, fc_bias, vectors):
+def feed_forward(x, cot, merged, out_all, fc_near, proj_near, fc_own, proj_own, small):
     rows, width = x.shape
-    group, part = fc_bias.shape[0], fc_near.shape[2]
+    group, part = small.shape[0], fc_near.shape[2]
     span = width // group
     f32, low = jnp.float32, jnp.bfloat16
     vmem = pl.BlockSpec(memory_space=pltpu.VMEM)
@@ -747,7 +761,6 @@
         in_specs=[
             vmem, vmem, vmem, vmem,
             hbm, hbm, hbm, hbm,
-            pl.BlockSpec((1, 1, part), lambda i: (i, 0, 0)),
             vmem,
         ],
         out_specs=[
@@ -769,6 +782,7 @@
             pltpu.VMEM((rows, width), f32),
             pltpu.VMEM((rows, width), f32),
             pltpu.VMEM((rows, 128), f32),
+            pltpu.VMEM((8, width), f32),
             pltpu.VMEM((rows, width), low),
             pltpu.VMEM((rows, width), f32),
             pltpu.VMEM((rows, width), f32),
@@ -794,11 +808,11 @@
         ],
         compiler_params=pltpu.CompilerParams(vmem_limit_bytes=62 * 2**20, collective_id=3, has_side_effects=True),
         name="feed_forward",
-    )(x, cot, merged, out_all, fc_near, proj_near, fc_own, proj_own, fc_bias, vectors)
+    )(x, cot, merged, out_all, fc_near, proj_near, fc_own, proj_own, small)
 
 
 def attend_back_kernel(
-    heads, group, qkv_ref, halo_ref, augk_ref, q2_ref, out_ref, grad_ref, kept, side,
+    heads, group, docs, qkv_ref, halo_ref, ids_ref, q2_ref, out_ref, grad_ref, kept, side,
     gqkv_ref, sums_ref,
     keys, values, keys_t, dkeys, dvalues, edge, ahead, mid, near, far, mine, met,
     edge_sems, load_sems, near_send, near_recv, far_send, far_recv,
@@ -866,8 +880,8 @@
         for load in loads():
             load.start()
         for s in range(seqs):
-            fill_keys(s, heads, halo_ref, augk_ref, 0, keys, values, None, keys_t)
-            fill_keys(s, heads, qkv_ref, augk_ref, WINDOW, keys, values, None, keys_t)
+            fill_keys(s, heads, halo_ref, ids_ref, docs, 0, keys, values, None, keys_t)
+            fill_keys(s, heads, qkv_ref, ids_ref, docs, WINDOW, keys, values, None, keys_t)
         dkeys[...] = jnp.zeros_like(dkeys)
         dvalues[...] = jnp.zeros_like(dvalues)
 
@@ -927,14 +941,14 @@
 
     @pl.when(step == last)
     def _():
+        def own(s, h, first, count):
+            span = slice(WINDOW + first, WINDOW + first + count)
+            return jnp.concatenate([dkeys[s * heads + h, span, :HD], dvalues[s * heads + h, span, :HD]], axis=1)
+
         for s in range(seqs):
             for h in range(heads):
                 c = h * 2 * HD
-                own = jnp.concatenate(
-                    [dkeys[s * heads + h, WINDOW:, :HD], dvalues[s * heads + h, WINDOW:, :HD]], axis=1
-                )
-                gqkv_ref[s, : rows - WINDOW, c : c + 2 * HD] = own[: rows - WINDOW].astype(low)
-                dkeys[s * heads + h, WINDOW:, :] = own
+                gqkv_ref[s, : rows - WINDOW, c : c + 2 * HD] = own(s, h, 0, rows - WINDOW).astype(low)
 
         @pl.when(line < line_end)
         def _():
@@ -948,9 +962,8 @@
         for s in range(seqs):
             for h in range(heads):
                 c = h * 2 * HD
-                own = dkeys[s * heads + h, rows:, :]
                 gqkv_ref[s, rows - WINDOW :, c : c + 2 * HD] = (
-                    own + ahead[s, :, c : c + 2 * HD].astype(f32)
+                    own(s, h, rows - WINDOW, WINDOW) + ahead[s, :, c : c + 2 * HD].astype(f32)
                 ).astype(low)
 
         for h in range(pieces):
@@ -969,9 +982,9 @@
                 edge_copy(s).wait_send()
 
 
-def attend_back(qkv, halo, augk, q2, out, grad, kept, side, heads, group):
+def attend_back(qkv, halo, ids, docs, q2, out, grad, kept, side, heads, group):
     seqs, rows, cols = qkv.shape
-    ext = augk.shape[1]
+    ext = ids.shape[1]
     half = group // 2
     f32, low = jnp.float32, jnp.bfloat16
     vmem = pl.BlockSpec(memory_space=pltpu.VMEM)
@@ -983,7 +996,7 @@
     edge = pltpu.VMEM((seqs, WINDOW, heads * 2 * HD), low)
     pair = pltpu.VMEM((2,) + part, low)
     return pl.pallas_call(
-        functools.partial(attend_back_kernel, heads, group),
+        functools.partial(attend_back_kernel, heads, group, docs),
         grid=(seqs * rows // BLK,),
         in_specs=[
             vmem, vmem, vmem,
@@ -1013,14 +1026,14 @@
         ],
         compiler_params=pltpu.CompilerParams(vmem_limit_bytes=62 * 2**20, collective_id=4, has_side_effects=True),
         name="attend_back",
-    )(qkv, halo, augk, q2, out, grad, kept, side)
+    )(qkv, halo, ids, q2, out, grad, kept, side)
 
 
 def finish_kernel(
     g_ref, wt_ref, x_ref, gres_ref, small_ref, sums_ref, out_kept, gvec_ref, gfcb_ref, z_hbm,
     input_grad_ref, fc_total_ref, proj_total_ref, out_total_ref, qkv_total_ref, vec_ref,
     z_all, odd, odd_in, even, mine, first_in, second_in, mt, rows6, vec_out, vec_in, vec_line,
-    acc, acc_out, acc_q, left, left_out, left_q, right, right_out, right_q, out_near, out_far, out_mid,
+    acc, acc_out, acc_q, left, left_out, left_q, right, right_out, right_q, total_q, out_near, out_far, out_mid,
     z_sem, odd_send, odd_recv, near_send, near_recv, far_send, far_recv,
     vec_send, vec_recv, vl_send, vl_recv, line_send, line_recv, out_send, out_recv,
 ):
@@ -1059,11 +1072,11 @@
         proj_chunks.append([r.at[1, part] for r in (sums_ref, acc, left, right)] + [there])
     cut = acc_q.shape[0] // 3
     qkv_chunks = [
-        [r.at[pl.ds(i * cut, cut)] for r in (acc_q, acc_q, left_q, right_q, qkv_total_ref)] for i in range(3)
+        [r.at[pl.ds(i * cut, cut)] for r in (acc_q, acc_q, left_q, right_q, total_q)] for i in range(3)
     ]
     out_chunk = [acc_out, acc_out, left_out, right_out, out_total_ref]
-    chunks = fc_chunks + proj_chunks[:1] + qkv_chunks + proj_chunks[1:] + [out_chunk]
-    early = 5
+    chunks = fc_chunks + proj_chunks[:2] + qkv_chunks + proj_chunks[2:] + [out_chunk]
+    early = 6
 
     def inwards(c):
         return remote(
@@ -1147,11 +1160,16 @@
     def odd_copy(j):
         return remote(odd.at[j], odd_in.at[j], odd_send.at[j], odd_recv.at[j], {"fsdp": at[1]})
 
-    for j in (3, 1, 2, 0):
+    def make_odd(j):
         for s in range(2):
             odd[j, s] = product(2 * j + 1, s).astype(low)
         odd_copy(j).start()
+
+    make_odd(3)
+    make_odd(1)
     advance(0, 1)
+    make_odd(2)
+    make_odd(0)
 
     def near_copy(s, i):
         j = 3 if i == 0 else 1 + s
@@ -1160,12 +1178,10 @@
     def far_copy(s):
         return remote(even.at[2 - s, s], second_in.at[s], far_send.at[s], far_recv.at[s], {"fsdp": ways[1 - s]})
 
-    for j in (3, 1, 2, 0):
+    def make_even(j):
+        odd_copy(j).wait_recv()
         for s in range(2):
-            part = product(2 * j, s)
-            if s == 0:
-                odd_copy(j).wait_recv()
-            part += odd_in[j, s].astype(f32)
+            part = product(2 * j, s) + odd_in[j, s].astype(f32)
             if j == 0:
                 mine[s] = part
             else:
@@ -1174,9 +1190,13 @@
                     near_copy(s, 0).start()
                 elif j == 1 + s:
                     near_copy(s, 1).start()
-        if j == 1:
-            advance(1, 2)
+
+    make_even(3)
+    advance(1, 2)
+    make_even(1)
+    make_even(2)
     advance(2, 3)
+    make_even(0)
 
     def wide(index):
         return jnp.concatenate([small_ref[f, index : index + 1, :] for f in range(group)], axis=1).astype(f32)
@@ -1195,16 +1215,17 @@
 
     column = lax.fori_loop(0, steps // 2, add_product, jnp.zeros((g_ref.shape[2], 128), f32))
     advance(3, 4)
-    column = lax.fori_loop(steps // 2, steps, add_product, column)
     for h in range(2):
         part = slice(h * out_cut, (h + 1) * out_cut)
         out_near_copy(2 * h + 1).wait_recv()
         out_mid[h] = (out_kept[2 - h, part].astype(f32) + out_near[h, 1].astype(f32)).astype(low)
         out_far_copy(h).start()
+    column = lax.fori_loop(steps // 2, steps, add_product, column)
     advance(4, 5)
     column = lax.fori_loop(steps, 2 * steps, add_product, column)
     acc_q[...] = mt[...].astype(low)
     begin(range(early, len(chunks) - 1))
+    advance(5, 6)
 
     def vec_copy(k):
         return remote(vec_out.at[k], vec_in.at[k], vec_send.at[k], vec_recv.at[k], {"fsdp": at[k]})
@@ -1214,7 +1235,6 @@
         even[2 - s, s] = (even[2 - s, s].astype(f32) + first_in[s, 0].astype(f32)).astype(low)
         far_copy(s).start()
 
-    advance(5, 6)
     for h in range(2):
         part = slice(h * out_cut, (h + 1) * out_cut)
         out_near_copy(2 * h).wait_recv()
@@ -1271,6 +1291,14 @@
         line_copy(d).wait_recv()
     vec_ref[...] = vec_line[0] + vec_line[1] + vec_line[2] + vec_line[3]
     advance(11, 12)
+    turned = total_q[...].T
+    pairs = heads * 2 * HD
+    turned = [
+        p
+        for h in range(heads)
+        for p in (turned[:, pairs + h * HD : pairs + (h + 1) * HD], turned[:, h * 2 * HD : (h + 1) * 2 * HD])
+    ]
+    qkv_total_ref[...] = jnp.concatenate(turned, axis=1)
     settle(11)
     receive(10)
     receive(11)
@@ -1321,7 +1349,7 @@
             jax.ShapeDtypeStruct(sums.shape[1:], low),
             jax.ShapeDtypeStruct((sums.shape[2], sums.shape[1]), low),
             jax.ShapeDtypeStruct(out_part, low),
-            jax.ShapeDtypeStruct(wt.shape, low),
+            jax.ShapeDtypeStruct(wt.shape[::-1], low),
             jax.ShapeDtypeStruct((16, span), f32),
         ],
         scratch_shapes=[
@@ -1339,6 +1367,7 @@
             pltpu.VMEM((4, 16, span), f32),
         ]
         + buffers * 3
+        + [pltpu.VMEM(wt.shape, low)]
         + [pltpu.VMEM((2, 2) + half_out, low), pltpu.VMEM((2,) + half_out, low), pltpu.VMEM((2,) + half_out, low)]
         + [dma, dma((4,)), dma((4,)), dma((2, 2)), dma((2, 2)), dma((2,)), dma((2,))]
         + [dma((group,)), dma((group,)), dma((3,)), dma((3,)), dma((3, 12)), dma((3, 12)), dma((6,)), dma((6,))],
@@ -1662,7 +1691,6 @@
     heads = qkv_weight.shape[1] // (3 * HD)
     docs = segment_ids.shape[1] // (2 * WINDOW)
     seq_index = lax.axis_index("seq")
-    me = lax.axis_index("fsdp")
     shard = norm1_gain.shape[0]
     f32, low = jnp.float32, jnp.bfloat16
 
@@ -1670,34 +1698,22 @@
     smalls = [v.reshape(-1, shard) for v in smalls]
     padded_ids = jnp.concatenate([jnp.full((seqs, WINDOW), -1, jnp.int32), segment_ids], axis=1)
     segment_ext = lax.dynamic_slice_in_dim(padded_ids, seq_index * part_rows, WINDOW + part_rows, 1)
-    augk, augq = mask_features(segment_ext, docs)
-    packed_weight = pack_columns(qkv_weight, heads)
-    head_bias = qv_bias.astype(f32)
-    head_bias = jnp.concatenate(
-        [head_bias[:, :HD], jnp.zeros((heads, HD), f32), head_bias[:, HD:]], axis=1
-    ).reshape(-1)
-    packed_bias = pack_columns(head_bias, heads)
-
+    ids = segment_ext[..., None]
     x = inputs.reshape(seqs * local_rows, width)
     cot = cotangent.reshape(seqs * local_rows, width)
-    all_small, z1, qkv = gather_project(x, smalls, packed_weight, packed_bias[None], group)
+    all_small, z1, qkv = gather_project(x, smalls, qkv_weight, qv_bias, group)
     head_out, q2, halo, merged, out_all, fc_near, proj_near = attend(
-        qkv, augk, augq, out_weight, fc_weight, proj_weight, heads, group
+        qkv, ids, docs, out_weight, fc_weight, proj_weight, heads, group
     )
-    full = lambda i: all_small[:, i].reshape(-1).astype(f32)
-    vectors = jnp.stack([full(2), full(3), full(4), full(5)] + [jnp.zeros((width,), f32)] * 4)
-    slots = jnp.stack([xor(me, r, group) for r in SLOT_AT])
-    fc_off = jnp.take(all_small[:, 6:10].reshape(group, -1), slots, axis=0).astype(f32)[:, None]
     layer_output, g_resid, g_heads, kept, side, out_kept, gvec, gfcb = feed_forward(
-        x, cot, merged.reshape(x.shape), out_all.reshape(width, width), fc_near, proj_near, fc_weight, proj_weight, fc_off, vectors
+        x, cot, merged.reshape(x.shape), out_all.reshape(width, width), fc_near, proj_near, fc_weight, proj_weight, all_small
     )
-    g_qkv, sums = attend_back(qkv, halo, augk, q2, head_out, g_heads, kept, side, heads, group)
+    g_qkv, sums = attend_back(qkv, halo, ids, docs, q2, head_out, g_heads, kept, side, heads, group)
     input_grad, fc_grad, proj_grad, out_grad, qkv_grad, vecs = finish(
-        g_qkv, packed_weight.T, x, g_resid, all_small, sums, out_kept, gvec, gfcb, z1
+        g_qkv, pack_columns(qkv_weight, heads).T, x, g_resid, all_small, sums, out_kept, gvec, gfcb, z1
     )
-    qkv_grad = unpack_columns(qkv_grad.T.astype(f32), heads)
     return (
-        layer_output.reshape(inputs.shape), input_grad.reshape(inputs.shape), vecs[0], vecs[1], qkv_grad,
+        layer_output.reshape(inputs.shape), input_grad.reshape(inputs.shape), vecs[0], vecs[1], qkv_grad.astype(f32),
         vecs[10 : 10 + heads], out_grad.astype(f32), vecs[2], vecs[3], vecs[4], fc_grad.astype(f32), vecs[6:10].reshape(-1),
         proj_grad.astype(f32), vecs[5],
     )

time: 377 us -> 356 us (0.944)
  Pallas kernels: 342 us -> 332 us
  other arithmetic: 14.8 us -> 7.51 us
  local copies, waits for them, and re-layouts: 14.9 us -> 9.43 us
    pallas_call x2, Pallas kernels: 128 us -> 121 us  [the longest x1 63 us: attend(): pl.pallas_call(functools.partial(attend_kernel, heads, group, docs), grid...]
where the time goes in v1:
time: 356 us; the launch traced here: 350 us
  Pallas kernels  332 us (93%)
  local copies, waits for them, and re-layouts  9.43 us (3%)
  other arithmetic  7.51 us (2%)
    pallas_call x1, Pallas kernels, finish(): pl.pallas_call(finish_kernel, in_specs=[vmem] * 9 + [pl.BlockSpec(memory_...  95.2 us
    pallas_call x1, Pallas kernels, feed_forward(): pl.pallas_call(functools.partial(feed_forward_kernel, group), grid=(group...  68.6 us
    pallas_call x1, Pallas kernels, attend(): pl.pallas_call(functools.partial(attend_kernel, heads, group, docs), grid...  63 us
    pallas_call x1, Pallas kernels, attend_back(): pl.pallas_call(functools.partial(attend_back_kernel, heads, group, docs),...  57.8 us
    pallas_call x1, Pallas kernels, gather_project(): pl.pallas_call(gather_project_kernel, in_specs=[vmem] * 10, out_specs=[vm...  47.1 us

profile of v1, /device:TPU:0, one launch (start us, length us, event | category | flops | bytes accessed | tf_op | source)
XLA Modules:
  0.0 349.8 jit_solution(12799142626333047944)
XLA Ops:
  0.6 0.0 copy-start.1
  0.8 0.9 fusion
  1.6 2.3 copy.31.ids_ref
  3.9 0.0 copy-done.7
  3.9 0.0 copy-done.8
  4.0 0.0 copy-done.9
  4.0 47.1 %gather_project.1 = (bf16[8,16,128]{2,1,0:T(8,128)(2,1)S(1)}, bf16[2,2048,1024]{2,1,0:T(8,128)(2,1)}, bf16[2,2048,384]{2,1,0:T(8,128)(2,1)S(1)}) custom-call(bf16[512,1024]{1,0:T(8,128)(2,1)S(1)} %bitcast.36, bf16[1,128]{1,0:T(2,128)(2,1)S(1)} %bitcast.38, bf16[1,128]{1,0:T(2,128)(2,1)S(1)} %bitcast.39, bf16[1,128]{1,0:T(2,128)(2,1)S(1)} %bitcast.40, ...), custom_call_target="tpu_custom_call" | custom-call | tf_op jit(solution)/shard_map/gather_project/pallas_call | solution.py:502
  51.1 1.6 copy-done
  52.8 0.6 copy-done.3
  53.4 63.0 %attend.1 = (bf16[2,2048,128]{2,1,0:T(8,128)(2,1)}, bf16[2,2,2048,128]{3,2,1,0:T(8,128)(2,1)}, bf16[2,1024,256]{2,1,0:T(8,128)(2,1)}, bf16[2,256,1024]{2,1,0:T(8...) custom-call(bf16[2,2048,384]{2,1,0:T(8,128)(2,1)} %copy-done, ...), custom_call_target="tpu_custom_call" | custom-call | tf_op jit(solution)/shard_map/attend/pallas_call | solution.py:344
  116.4 68.6 %feed_forward.1 = (bf16[512,1024]{1,0:T(8,128)(2,1)}, f32[512,1024]{1,0:T(8,128)}, bf16[2,2048,128]{2,1,0:T(8,128)(2,1)}, bf16[4,2,1024,512]{3,2,1,0:T(8,128)(2,...) custom-call(bf16[512,1024]{1,0:T(8,128)(2,1)} %bitcast.34, ...), custom_call_target="tpu_custom_call" | custom-call | tf_op jit(solution)/shard_map/feed_forward/pallas_call | solution.py:758
  185.0 57.8 %attend_back.1 = (bf16[2,2048,384]{2,1,0:T(8,128)(2,1)}, bf16[2,1024,512]{2,1,0:T(8,128)(2,1)}) custom-call(bf16[2,2048,384]{2,1,0:T(8,128)(2,1)} %copy-done, bf16[2,1024,256]{2,1,0:T(8,128)(2,1)} %get-tuple-element.47.halo_ref, s32[2,3072,1]{2,1,0:T(8,128)} %copy.31.ids_ref, bf16[2,2,2048,128]{3,2,1,0:T(8,128)(2,1)} %get-tuple-element.48.q2_ref, ...), custom_call_target="tpu_custom_call" | custom-call | tf_op jit(solution)/shard_map/attend_back/pallas_call | solution.py:998
  242.8 0.3 copy.33
  243.2 0.9 maximum_bitcast_fusion.wt_ref
  244.1 95.2 %finish.1 = (bf16[512,1024]{1,0:T(8,128)(2,1)}, bf16[1024,512]{1,0:T(8,128)(2,1)}, bf16[512,1024]{1,0:T(8,128)(2,1)}, bf16[128,1024]{1,0:T(8,128)(2,1)}, bf16[1024,384]{1,0:T(8,128)(2,1)}, /*index=5*/f32[16,128]{1,0:T(8,128)}) custom-call(bf16[2,2048,384]{2,1,0:T(8,128)(2,1)} %get-tuple-element.53.g_ref, bf16[384,1024]{1,0:T(8,128)(2,1)} %maximum_bitcast_fusion.wt_ref, ...), custom_call_target="tpu_custom_call" | custom-call | tf_op jit(solution)/shard_map/finish/pallas_call | solution.py:1343
  339.4 2.9 convert_element_type.14
  342.3 1.6 convert_element_type.15
  343.9 1.2 convert_element_type.12
  345.1 0.8 convert_element_type.13
  346.0 0.5 slice_bitcast_fusion.1
  346.5 0.6 slice_bitcast_fusion
  347.1 0.6 slice.34
  347.7 1.0 copy.36
  348.6 1.0 copy.37
  (32 shorter events, 0.1 us)
Async XLA Ops:
  0.6 3.3 copy-start.1
  0.7 3.3 copy-start.5
  0.7 3.3 copy-start.6
  0.7 3.3 copy-start.7
  0.7 3.3 copy-start.8
  0.7 3.3 copy-start.9
  0.7 3.3 copy-start.10
  0.7 3.3 copy-start.4
  0.7 3.3 copy-start.2
  0.7 3.3 copy-start.11
  51.1 1.6 copy-start
  52.8 0.6 copy-start.3
  339.4 2.9 copy-start.12
  342.3 1.6 copy-start.15
  342.3 2.8 copy-start.16
  343.9 2.1 copy-start.17
  343.9 3.8 %copy-start.13 = (bf16[512,1024]{1,0:T(8,128)(2,1)S(1)}, bf16[512,1024]{1,0:T(8,128)(2,1)}, u32[]{:S(2)}) copy-start(bf16[512,1024]{1,0:T(8,128)(2,1)} %get-tuple-element.46) | copy-start | bytes 3145732
  343.9 4.8 %copy-start.14 = (bf16[512,1024]{1,0:T(8,128)(2,1)S(1)}, bf16[512,1024]{1,0:T(8,128)(2,1)}, u32[]{:S(2)}) copy-start(bf16[512,1024]{1,0:T(8,128)(2,1)} %get-tuple-element.60) | copy-start | bytes 3145732

commit v2 on v1

--- a/solution.py
+++ b/solution.py
@@ -86,9 +86,9 @@
 
 
 def attend_kernel(
-    heads, group, docs, qkv_ref, ids_ref, out_w, fc_w, proj_w,
+    heads, group, docs, qkv_hbm, ids_hbm, out_w, fc_w, proj_w,
     out_ref, q2_ref, halo_ref, merged_ref, out_all, fc_all, proj_all,
-    keys, values, values_t, sent, behind, own_sems, send_sems, recv_sems, halo_sems, w_own, w_send, w_recv,
+    qkv_ref, ids_ref, in_sems, keys, values, values_t, sent, behind, own_sems, send_sems, recv_sems, halo_sems, w_own, w_send, w_recv,
 ):
     step = pl.program_id(0)
     last = pl.num_programs(0) - 1
@@ -106,7 +106,7 @@
 
     def halo_copy():
         return pltpu.make_async_remote_copy(
-            src_ref=qkv_ref.at[:, pl.ds(rows - WINDOW, WINDOW), pl.ds(0, width)],
+            src_ref=qkv_hbm.at[:, pl.ds(rows - WINDOW, WINDOW), pl.ds(0, width)],
             dst_ref=behind, send_sem=halo_sems.at[0], recv_sem=halo_sems.at[1],
             device_id={"seq": lax.rem(line + 1, line_end + 1)}, device_id_type=MESH,
         )
@@ -163,6 +163,12 @@
 
     @pl.when(step == 0)
     def _():
+        loads = [
+            pltpu.make_async_copy(qkv_hbm, qkv_ref, in_sems.at[0]),
+            pltpu.make_async_copy(ids_hbm, ids_ref, in_sems.at[1]),
+        ]
+        for load in loads:
+            load.start()
         barrier = pltpu.get_barrier_semaphore()
         for peer in at[1:]:
             pl.semaphore_signal(barrier, inc=1, device_id={"fsdp": peer}, device_id_type=MESH)
@@ -183,6 +189,8 @@
             p_near(r).start()
         w_copy(2, 1).start()
         w_keep(0).start()
+        for load in loads:
+            load.wait()
         for s in range(seqs):
             fill_keys(s, heads, qkv_ref, ids_ref, docs, WINDOW, keys, values, values_t, None)
 
@@ -344,7 +352,7 @@
     return pl.pallas_call(
         functools.partial(attend_kernel, heads, group, docs),
         grid=(seqs * rows // BLK,),
-        in_specs=[vmem] * 2 + [hbm] * 3,
+        in_specs=[hbm] * 5,
         out_specs=[vmem] * 3 + [hbm] * 4,
         out_shape=[
             jax.ShapeDtypeStruct((seqs, rows, heads * HD), low),
@@ -354,6 +362,9 @@
         ]
         + [jax.ShapeDtypeStruct((n,) + w.shape, low) for n, w in ((group, out_w), (NEAR - 1, fc_w), (NEAR - 1, proj_w))],
         scratch_shapes=[
+            pltpu.VMEM(qkv.shape, low),
+            pltpu.VMEM(ids.shape, jnp.int32),
+            pltpu.SemaphoreType.DMA((2,)),
             pltpu.VMEM((every, ext, 2 * HD), low),
             pltpu.VMEM((every, ext, 2 * HD), low),
             pltpu.VMEM((every, 2 * HD, ext), low),
@@ -441,14 +452,15 @@
         made = jnp.concatenate([h[:, HD:] for h in head] + [h[:, :HD] for h in head], axis=1)
         qkv_ref[s, pl.ds(start, rows), :] = made
 
-    for s in range(2):
-        z1[s * rows : (s + 1) * rows, :] = standardize(x_ref[s * rows : (s + 1) * rows, :].astype(f32))[0]
+    z1[...] = standardize(x_ref[:rows, :].astype(f32))[0]
     for k in range(1, group):
         small_copy(k).wait()
     gain = jnp.concatenate([smalls[f, 0:1, :] for f in range(group)], axis=1).astype(f32)
     offset = jnp.concatenate([smalls[f, 1:2, :] for f in range(group)], axis=1).astype(f32)
     for s in range(2):
-        pieces[me, s] = (z1[s * rows : (s + 1) * rows, :] * gain + offset).astype(low)
+        if s == 1:
+            z1[...] = standardize(x_ref[rows:, :].astype(f32))[0]
+        pieces[me, s] = (z1[...] * gain + offset).astype(low)
         move(2, s).start()
         move(4, s).start()
         move(1, s).start()
@@ -509,7 +521,7 @@
             jax.ShapeDtypeStruct((2, group * half, cols), low),
         ],
         scratch_shapes=[
-            pltpu.VMEM((rows, width), jnp.float32),
+            pltpu.VMEM((half, width), jnp.float32),
             pltpu.VMEM((group, 2, half, width), low),
             pltpu.VMEM((group, 16, span), low),
             pltpu.VMEM((16, span), low),
@@ -540,9 +552,9 @@
 
 
 def feed_forward_kernel(
-    group, x_ref, cot_ref, merged_ref, out_ref, fc_near, proj_near, fc_own, proj_own, small_ref,
+    group, x_hbm, cot_hbm, merged_hbm, out_hbm, fc_near, proj_near, fc_own, proj_own, small_ref,
     layer_ref, gres_ref, gheads_ref, keep_ref, side_ref, gout_ref, gvec_ref, gfcb_ref,
-    resid, z2, rate, vec_ref, normed, total, gnormed, fc_w, proj_w, given, taken, gmerged, gout_given, gout_taken,
+    x_ref, cot_ref, merged_ref, out_ref, in_sems, resid, z2, rate, vec_ref, normed, total, gnormed, fc_w, proj_w, given, taken, gmerged, gout_given, gout_taken,
     load_sems, far_send, far_recv, pair_send, pair_recv, side_send, side_recv, keep_sems, head_send, head_recv,
     own_sem, gout_sems,
 ):
@@ -550,7 +562,7 @@
     last = group - 1
     me = lax.axis_index("fsdp")
     at = [xor(me, k, group) for k in range(group)]
-    rows = x_ref.shape[0]
+    rows = x_hbm.shape[0]
     block = rows // 2
     f32, low = jnp.float32, jnp.bfloat16
     span = merged_ref.shape[1] // group
@@ -610,12 +622,22 @@
 
     @pl.when(step == 0)
     def _():
+        brought = [
+            pltpu.make_async_copy(src, dst, in_sems.at[i])
+            for i, (src, dst) in enumerate(
+                ((merged_hbm, merged_ref), (out_hbm, out_ref), (x_hbm, x_ref), (cot_hbm, cot_ref))
+            )
+        ]
+        for copy in brought:
+            copy.start()
         enter(at[1:])
         for a in range(2):
             load(a, 0).start()
         for a in range(2):
             far_copy(a, 0).start()
             far_copy(a, 1).start()
+        for copy in brought:
+            copy.wait()
         for i in range(4):
             vec_ref[i : i + 1, :] = jnp.concatenate(
                 [small_ref[f, 2 + i : 3 + i, :] for f in range(group)], axis=1
@@ -759,7 +781,7 @@
         functools.partial(feed_forward_kernel, group),
         grid=(group,),
         in_specs=[
-            vmem, vmem, vmem, vmem,
+            hbm, hbm, hbm, hbm,
             hbm, hbm, hbm, hbm,
             vmem,
         ],
@@ -779,6 +801,11 @@
             jax.ShapeDtypeStruct((group, 1, part), f32),
         ],
         scratch_shapes=[
+            pltpu.VMEM((rows, width), low),
+            pltpu.VMEM((rows, width), low),
+            pltpu.VMEM((rows, width), low),
+            pltpu.VMEM((width, width), low),
+            pltpu.SemaphoreType.DMA((4,)),
             pltpu.VMEM((rows, width), f32),
             pltpu.VMEM((rows, width), f32),
             pltpu.VMEM((rows, 128), f32),
@@ -812,9 +839,9 @@
 
 
 def attend_back_kernel(
-    heads, group, docs, qkv_ref, halo_ref, ids_ref, q2_ref, out_ref, grad_ref, kept, side,
+    heads, group, docs, qkv_hbm, halo_hbm, ids_hbm, q2_ref, out_ref, grad_ref, kept, side,
     gqkv_ref, sums_ref,
-    keys, values, keys_t, dkeys, dvalues, edge, ahead, mid, near, far, mine, met,
+    qkv_ref, halo_ref, ids_ref, in_sems, keys, values, keys_t, dkeys, dvalues, edge, ahead, mid, near, far, mine, met,
     edge_sems, load_sems, near_send, near_recv, far_send, far_recv,
 ):
     step = pl.program_id(0)
@@ -823,7 +850,7 @@
     line = lax.axis_index("seq")
     line_end = lax.axis_size("seq") - 1
     at = [xor(me, k, group) for k in range(group)]
-    seqs, rows = qkv_ref.shape[0], qkv_ref.shape[1]
+    seqs, rows = qkv_hbm.shape[0], qkv_hbm.shape[1]
     half = group // 2
     seq = lax.rem(lax.div(step, half), 2)
     place = lax.div(step, group) * half + lax.rem(step, half)
@@ -867,6 +894,14 @@
 
     @pl.when(step == 0)
     def _():
+        brought = [
+            pltpu.make_async_copy(src, dst, in_sems.at[i])
+            for i, (src, dst) in enumerate(((qkv_hbm, qkv_ref), (halo_hbm, halo_ref), (ids_hbm, ids_ref)))
+        ]
+        for load in brought:
+            load.start()
+        dkeys[...] = jnp.zeros_like(dkeys)
+        dvalues[...] = jnp.zeros_like(dvalues)
         barrier = pltpu.get_barrier_semaphore()
         for peer in (at[2], at[4]):
             pl.semaphore_signal(barrier, inc=1, device_id={"fsdp": peer}, device_id_type=MESH)
@@ -879,11 +914,11 @@
                 near_copy(a, h).start()
         for load in loads():
             load.start()
+        for load in brought:
+            load.wait()
         for s in range(seqs):
             fill_keys(s, heads, halo_ref, ids_ref, docs, 0, keys, values, None, keys_t)
             fill_keys(s, heads, qkv_ref, ids_ref, docs, WINDOW, keys, values, None, keys_t)
-        dkeys[...] = jnp.zeros_like(dkeys)
-        dvalues[...] = jnp.zeros_like(dvalues)
 
     for s in range(seqs):
         @pl.when((step == (s + 1) * half) & (line > 0))
@@ -999,7 +1034,7 @@
         functools.partial(attend_back_kernel, heads, group, docs),
         grid=(seqs * rows // BLK,),
         in_specs=[
-            vmem, vmem, vmem,
+            hbm, hbm, hbm,
             pl.BlockSpec((1, heads, BLK, 2 * HD), lambda i: (seq_of(i), 0, place_of(i), 0)),
             pl.BlockSpec((1, BLK, heads * HD), lambda i: (seq_of(i), place_of(i), 0)),
             pl.BlockSpec((1, BLK, heads * HD), lambda i: (seq_of(i), place_of(i), 0)),
@@ -1011,6 +1046,10 @@
             jax.ShapeDtypeStruct((2,) + part, low),
         ],
         scratch_shapes=[
+            pltpu.VMEM(qkv.shape, low),
+            pltpu.VMEM(halo.shape, low),
+            pltpu.VMEM(ids.shape, jnp.int32),
+            pltpu.SemaphoreType.DMA((3,)),
             pltpu.VMEM((every, ext, 2 * HD), low),
             pltpu.VMEM((every, ext, 2 * HD), low),
             pltpu.VMEM((every, 2 * HD, ext), low),
@@ -1030,9 +1069,9 @@
 
 
 def finish_kernel(
-    g_ref, wt_ref, x_ref, gres_ref, small_ref, sums_ref, out_kept, gvec_ref, gfcb_ref, z_hbm,
+    g_hbm, wt_hbm, x_hbm, gres_hbm, small_ref, sums_hbm, out_hbm, gvec_ref, gfcb_ref, z_hbm,
     input_grad_ref, fc_total_ref, proj_total_ref, out_total_ref, qkv_total_ref, vec_ref,
-    z_all, odd, odd_in, even, mine, first_in, second_in, mt, rows6, vec_out, vec_in, vec_line,
+    g_ref, wt_ref, x_ref, gres_ref, sums_ref, out_kept, in_sems, z_all, odd, odd_in, even, mine, first_in, second_in, mt, rows6, vec_out, vec_in, vec_line,
     acc, acc_out, acc_q, left, left_out, left_q, right, right_out, right_q, total_q, out_near, out_far, out_mid,
     z_sem, odd_send, odd_recv, near_send, near_recv, far_send, far_recv,
     vec_send, vec_recv, vl_send, vl_recv, line_send, line_recv, out_send, out_recv,
@@ -1042,11 +1081,11 @@
     line = lax.axis_index("seq")
     line_size = 4
     at = [xor(me, k, group) for k in range(group)]
-    block = x_ref.shape[0] // 2
+    block = x_hbm.shape[0] // 2
     f32, low = jnp.float32, jnp.bfloat16
-    width = x_ref.shape[1]
+    width = x_hbm.shape[1]
     span = small_ref.shape[2]
-    heads = wt_ref.shape[0] // (3 * HD)
+    heads = wt_hbm.shape[0] // (3 * HD)
     outer = (line == 0) | (line == line_size - 1)
     inner = (line > 0) & (line < line_size - 1)
 
@@ -1055,6 +1094,17 @@
             src_ref=src, dst_ref=dst, send_sem=send, recv_sem=recv, device_id=to, device_id_type=MESH
         )
 
+    brought = [
+        pltpu.make_async_copy(src, dst, in_sems.at[i])
+        for i, (src, dst) in enumerate(
+            (
+                (g_hbm, g_ref), (wt_hbm, wt_ref), (sums_hbm, sums_ref), (out_hbm, out_kept), (x_hbm, x_ref),
+                (gres_hbm, gres_ref),
+            )
+        )
+    ]
+    for copy in brought:
+        copy.start()
     barrier = pltpu.get_barrier_semaphore()
     for peer in at[1:]:
         pl.semaphore_signal(barrier, inc=1, device_id={"fsdp": peer}, device_id_type=MESH)
@@ -1063,19 +1113,23 @@
         pl.semaphore_signal(barrier, inc=1, device_id={"seq": other}, device_id_type=MESH)
     pl.semaphore_wait(barrier, group - 1 + line_size - 1)
 
-    cut = sums_ref.shape[1] // 4
+    cut = sums_hbm.shape[1] // 4
     fc_chunks, proj_chunks = [], []
     for i in range(4):
         part = pl.ds(i * cut, cut)
-        fc_chunks.append([r.at[0, part] for r in (sums_ref, acc, left, right)] + [fc_total_ref.at[part]])
+        fc_chunks.append([r.at[0, part] for r in (sums_hbm, acc, left, right)] + [fc_total_ref.at[part], sums_ref.at[0, part]])
         there = proj_total_ref.at[pl.ds(i % 2 * cut, cut), pl.ds(i // 2 * sums_ref.shape[2], sums_ref.shape[2])]
-        proj_chunks.append([r.at[1, part] for r in (sums_ref, acc, left, right)] + [there])
+        proj_chunks.append([r.at[1, part] for r in (sums_hbm, acc, left, right)] + [there, sums_ref.at[1, part]])
     cut = acc_q.shape[0] // 3
     qkv_chunks = [
-        [r.at[pl.ds(i * cut, cut)] for r in (acc_q, acc_q, left_q, right_q, total_q)] for i in range(3)
+        [r.at[pl.ds(i * cut, cut)] for r in (acc_q, acc_q, left_q, right_q, total_q, acc_q)] for i in range(3)
     ]
-    out_chunk = [acc_out, acc_out, left_out, right_out, out_total_ref]
-    chunks = fc_chunks + proj_chunks[:2] + qkv_chunks + proj_chunks[2:] + [out_chunk]
+    cut = acc_out.shape[0] // 2
+    out_chunks = [
+        [r.at[pl.ds(i * cut, cut)] for r in (acc_out, acc_out, left_out, right_out, out_total_ref, acc_out)]
+        for i in range(2)
+    ]
+    chunks = fc_chunks + proj_chunks[:2] + qkv_chunks + proj_chunks[2:] + out_chunks
     early = 6
 
     def inwards(c):
@@ -1104,7 +1158,7 @@
         @pl.when(inner)
         def _():
             inwards(c).wait_recv()
-            own, acc_c, left_c = chunks[c][:3]
+            acc_c, left_c, own = chunks[c][1], chunks[c][2], chunks[c][5]
             acc_c[...] = (own[...].astype(f32) + left_c[...].astype(f32)).astype(low)
             across(c).start()
 
@@ -1134,13 +1188,13 @@
     load.start()
 
     ways = (at[2], at[4])
-    out_cut = out_kept.shape[1] // 2
+    out_cut = out_hbm.shape[1] // 2
     out_first = ((0, 1, 0), (0, 3, 1), (1, 2, 0), (1, 3, 1))
 
     def out_near_copy(n):
         h, slot, j = out_first[n]
         return pltpu.make_async_remote_copy(
-            src_ref=out_kept.at[slot, pl.ds(h * out_cut, out_cut)], dst_ref=out_near.at[h, j], send_sem=out_send.at[n],
+            src_ref=out_hbm.at[slot, pl.ds(h * out_cut, out_cut)], dst_ref=out_near.at[h, j], send_sem=out_send.at[n],
             recv_sem=out_recv.at[n], device_id={"fsdp": ways[h]}, device_id_type=MESH,
         )
 
@@ -1165,6 +1219,8 @@
             odd[j, s] = product(2 * j + 1, s).astype(low)
         odd_copy(j).start()
 
+    for copy in brought:
+        copy.wait()
     make_odd(3)
     make_odd(1)
     advance(0, 1)
@@ -1221,19 +1277,19 @@
         out_mid[h] = (out_kept[2 - h, part].astype(f32) + out_near[h, 1].astype(f32)).astype(low)
         out_far_copy(h).start()
     column = lax.fori_loop(steps // 2, steps, add_product, column)
-    advance(4, 5)
-    column = lax.fori_loop(steps, 2 * steps, add_product, column)
-    acc_q[...] = mt[...].astype(low)
-    begin(range(early, len(chunks) - 1))
-    advance(5, 6)
-
-    def vec_copy(k):
-        return remote(vec_out.at[k], vec_in.at[k], vec_send.at[k], vec_recv.at[k], {"fsdp": at[k]})
-
     for s in range(2):
         near_copy(s, 0).wait_recv()
         even[2 - s, s] = (even[2 - s, s].astype(f32) + first_in[s, 0].astype(f32)).astype(low)
         far_copy(s).start()
+
+    advance(4, 5)
+    column = lax.fori_loop(steps, 2 * steps, add_product, column)
+    acc_q[...] = mt[...].astype(low)
+    begin(range(early, len(chunks) - 2))
+    advance(5, 6)
+
+    def vec_copy(k):
+        return remote(vec_out.at[k], vec_in.at[k], vec_send.at[k], vec_recv.at[k], {"fsdp": at[k]})
 
     for h in range(2):
         part = slice(h * out_cut, (h + 1) * out_cut)
@@ -1242,7 +1298,7 @@
         acc_out[part] = (
             out_kept[0, part].astype(f32) + out_near[h, 0].astype(f32) + out_far[h].astype(f32)
         ).astype(low)
-    begin([len(chunks) - 1])
+    begin([len(chunks) - 2, len(chunks) - 1])
 
     def line_copy(d):
         return remote(vec_line.at[line], vec_line.at[line], vl_send.at[d], vl_recv.at[d], {"seq": others[d]})
@@ -1290,7 +1346,7 @@
     for d in range(line_size - 1):
         line_copy(d).wait_recv()
     vec_ref[...] = vec_line[0] + vec_line[1] + vec_line[2] + vec_line[3]
-    advance(11, 12)
+    advance(11, 13)
     turned = total_q[...].T
     pairs = heads * 2 * HD
     turned = [
@@ -1299,9 +1355,9 @@
         for p in (turned[:, pairs + h * HD : pairs + (h + 1) * HD], turned[:, h * 2 * HD : (h + 1) * 2 * HD])
     ]
     qkv_total_ref[...] = jnp.concatenate(turned, axis=1)
-    settle(11)
-    receive(10)
+    settle(12)
     receive(11)
+    receive(12)
     for j in range(4):
         odd_copy(j).wait_send()
     for s in range(2):
@@ -1336,13 +1392,14 @@
     span = small.shape[2]
     f32, low = jnp.float32, jnp.bfloat16
     vmem = pl.BlockSpec(memory_space=pltpu.VMEM)
+    hbm = pl.BlockSpec(memory_space=pl.ANY)
     dma = pltpu.SemaphoreType.DMA
     out_part = out_kept.shape[1:]
     half_out = (out_part[0] // 2, out_part[1])
     buffers = [pltpu.VMEM(sums.shape, low), pltpu.VMEM(out_part, low), pltpu.VMEM(wt.shape, low)]
     return pl.pallas_call(
         finish_kernel,
-        in_specs=[vmem] * 9 + [pl.BlockSpec(memory_space=pl.ANY)],
+        in_specs=[hbm] * 4 + [vmem, hbm, hbm, vmem, vmem, hbm],
         out_specs=[vmem] * 6,
         out_shape=[
             jax.ShapeDtypeStruct((rows, width), low),
@@ -1353,6 +1410,13 @@
             jax.ShapeDtypeStruct((16, span), f32),
         ],
         scratch_shapes=[
+            pltpu.VMEM(g.shape, low),
+            pltpu.VMEM(wt.shape, low),
+            pltpu.VMEM(x.shape, low),
+            pltpu.VMEM(gres.shape, f32),
+            pltpu.VMEM(sums.shape, low),
+            pltpu.VMEM(out_kept.shape, low),
+            dma((6,)),
             pltpu.VMEM(z_all.shape, low),
             pltpu.VMEM((group // 2, 2, half, width), low),
             pltpu.VMEM((group // 2, 2, half, width), low),
@@ -1370,7 +1434,7 @@
         + [pltpu.VMEM(wt.shape, low)]
         + [pltpu.VMEM((2, 2) + half_out, low), pltpu.VMEM((2,) + half_out, low), pltpu.VMEM((2,) + half_out, low)]
         + [dma, dma((4,)), dma((4,)), dma((2, 2)), dma((2, 2)), dma((2,)), dma((2,))]
-        + [dma((group,)), dma((group,)), dma((3,)), dma((3,)), dma((3, 12)), dma((3, 12)), dma((6,)), dma((6,))],
+        + [dma((group,)), dma((group,)), dma((3,)), dma((3,)), dma((3, 13)), dma((3, 13)), dma((6,)), dma((6,))],
         compiler_params=pltpu.CompilerParams(vmem_limit_bytes=62 * 2**20, collective_id=5, has_side_effects=True),
         name="finish",
     )(g, wt, x, gres, small, sums, out_kept, gvec, gfcb, z_all)

time: 356 us -> 346 us (0.972)
  Pallas kernels: 332 us -> 321 us
    pallas_call x1, Pallas kernels: 95.2 us -> 90.8 us  [finish(): pl.pallas_call(finish_kernel, in_specs=[hbm] * 4 + [vmem, hbm, hbm, vmem,...]
where the time goes in v2:
time: 346 us; the launch traced here: 339 us
  Pallas kernels  321 us (93%)
  local copies, waits for them, and re-layouts  9.43 us (3%)
  other arithmetic  7.51 us (2%)
    pallas_call x1, Pallas kernels, finish(): pl.pallas_call(finish_kernel, in_specs=[hbm] * 4 + [vmem, hbm, hbm, vmem,...  90.8 us
    pallas_call x1, Pallas kernels, feed_forward(): pl.pallas_call(functools.partial(feed_forward_kernel, group), grid=(group...  66.9 us
    pallas_call x1, Pallas kernels, attend(): pl.pallas_call(functools.partial(attend_kernel, heads, group, docs), grid...  60.2 us
    pallas_call x1, Pallas kernels, attend_back(): pl.pallas_call(functools.partial(attend_back_kernel, heads, group, docs),...  56.3 us
    pallas_call x1, Pallas kernels, gather_project(): pl.pallas_call(gather_project_kernel, in_specs=[vmem] * 10, out_specs=[vm...  47.1 us

profile of v2, /device:TPU:0, one launch (start us, length us, event | category | flops | bytes accessed | tf_op | source)
XLA Modules:
  0.0 339.3 jit_solution(12514660988887489975)
XLA Ops:
  0.6 0.0 copy-start.1
  0.8 0.9 fusion
  1.6 2.3 copy.31.ids_hbm
  3.9 0.0 copy-done.1
  3.9 0.0 copy-done.6
  4.0 47.1 %gather_project.1 = (bf16[8,16,128]{2,1,0:T(8,128)(2,1)S(1)}, bf16[2,2048,1024]{2,1,0:T(8,128)(2,1)}, bf16[2,2048,384]{2,1,0:T(8,128)(2,1)S(1)}) custom-call(bf16[512,1024]{1,0:T(8,128)(2,1)S(1)} %bitcast.36, bf16[1,128]{1,0:T(2,128)(2,1)S(1)} %bitcast.38, bf16[1,128]{1,0:T(2,128)(2,1)S(1)} %bitcast.39, bf16[1,128]{1,0:T(2,128)(2,1)S(1)} %bitcast.40, ...), custom_call_target="tpu_custom_call" | custom-call | tf_op jit(solution)/shard_map/gather_project/pallas_call | solution.py:514
  51.2 1.6 copy-done
  52.8 0.6 copy-done.3
  53.4 60.2 %attend.1 = (bf16[2,2048,128]{2,1,0:T(8,128)(2,1)}, bf16[2,2,2048,128]{3,2,1,0:T(8,128)(2,1)}, bf16[2,1024,256]{2,1,0:T(8,128)(2,1)}, bf16[2,256,1024]{2,1,0:T(8...) custom-call(bf16[2,2048,384]{2,1,0:T(8,128)(2,1)} %copy-done, ...), custom_call_target="tpu_custom_call" | custom-call | tf_op jit(solution)/shard_map/attend/pallas_call | solution.py:352
  113.6 66.9 %feed_forward.1 = (bf16[512,1024]{1,0:T(8,128)(2,1)}, f32[512,1024]{1,0:T(8,128)}, bf16[2,2048,128]{2,1,0:T(8,128)(2,1)}, bf16[4,2,1024,512]{3,2,1,0:T(8,128)(2,...) custom-call(bf16[512,1024]{1,0:T(8,128)(2,1)} %bitcast.34, ...), custom_call_target="tpu_custom_call" | custom-call | tf_op jit(solution)/shard_map/feed_forward/pallas_call | solution.py:780
  180.5 56.3 %attend_back.1 = (bf16[2,2048,384]{2,1,0:T(8,128)(2,1)}, bf16[2,1024,512]{2,1,0:T(8,128)(2,1)}) custom-call(bf16[2,2048,384]{2,1,0:T(8,128)(2,1)} %copy-done, bf16[2,1024,256]{2,1,0:T(8,128)(2,1)} %get-tuple-element.47.halo_hbm, s32[2,3072,1]{2,1,0:T(8,128)} %copy.31.ids_hbm, bf16[2,2,2048,128]{3,2,1,0:T(8,128)(2,1)} %get-tuple-element.48.q2_ref, ...), custom_call_target="tpu_custom_call" | custom-call | tf_op jit(solution)/shard_map/attend_back/pallas_call | solution.py:1033
  236.8 0.3 copy.33
  237.2 0.9 maximum_bitcast_fusion.wt_hbm
  238.1 90.8 %finish.1 = (bf16[512,1024]{1,0:T(8,128)(2,1)}, bf16[1024,512]{1,0:T(8,128)(2,1)}, bf16[512,1024]{1,0:T(8,128)(2,1)}, bf16[128,1024]{1,0:T(8,128)(2,1)}, bf16[1024,384]{1,0:T(8,128)(2,1)}, /*index=5*/f32[16,128]{1,0:T(8,128)}) custom-call(bf16[2,2048,384]{2,1,0:T(8,128)(2,1)} %get-tuple-element.53.g_hbm, bf16[384,1024]{1,0:T(8,128)(2,1)} %maximum_bitcast_fusion.wt_hbm, ...), custom_call_target="tpu_custom_call" | custom-call | tf_op jit(solution)/shard_map/finish/pallas_call | solution.py:1400
  328.9 2.9 convert_element_type.14
  331.8 1.6 convert_element_type.15
  333.4 0.0 copy-done.15
  333.4 1.2 convert_element_type.12
  334.7 0.8 convert_element_type.13
  335.5 0.5 slice_bitcast_fusion.1
  336.0 0.6 slice_bitcast_fusion
  336.6 0.6 slice.34
  337.2 1.0 copy.36
  338.2 1.0 copy.37
  (32 shorter events, 0.1 us)
Async XLA Ops:
  0.6 3.3 copy-start.1
  0.7 3.3 copy-start.5
  0.7 3.3 copy-start.6
  0.7 3.3 copy-start.7
  0.7 3.3 copy-start.8
  0.7 3.3 copy-start.9
  0.7 3.3 copy-start.10
  0.7 3.3 copy-start.4
  0.7 3.3 copy-start.2
  0.7 3.3 copy-start.11
  51.1 1.6 copy-start
  52.8 0.6 copy-start.3
  328.9 2.9 copy-start.12
  331.8 1.6 copy-start.15
  331.8 2.8 copy-start.16
  333.4 2.1 copy-start.17
  333.4 3.8 %copy-start.13 = (bf16[512,1024]{1,0:T(8,128)(2,1)S(1)}, bf16[512,1024]{1,0:T(8,128)(2,1)}, u32[]{:S(2)}) copy-start(bf16[512,1024]{1,0:T(8,128)(2,1)} %get-tuple-element.46) | copy-start | bytes 3145732
  333.4 4.8 %copy-start.14 = (bf16[512,1024]{1,0:T(8,128)(2,1)S(1)}, bf16[512,1024]{1,0:T(8,128)(2,1)}, u32[]{:S(2)}) copy-start(bf16[512,1024]{1,0:T(8,128)(2,1)} %get-tuple-element.60) | copy-start | bytes 3145732

commit v3 on v2

--- a/solution.py
+++ b/solution.py
@@ -86,8 +86,8 @@
 
 
 def attend_kernel(
-    heads, group, docs, qkv_hbm, ids_hbm, out_w, fc_w, proj_w,
-    out_ref, q2_ref, halo_ref, merged_ref, out_all, fc_all, proj_all,
+    heads, group, docs, qkv_hbm, row_ref, out_w, fc_w, proj_w,
+    out_ref, q2_ref, halo_ref, merged_ref, out_all, fc_all, proj_all, ids_out,
     qkv_ref, ids_ref, in_sems, keys, values, values_t, sent, behind, own_sems, send_sems, recv_sems, halo_sems, w_own, w_send, w_recv,
 ):
     step = pl.program_id(0)
@@ -161,14 +161,13 @@
             w_copy(a, 6).start()
             w_copy(a, 6, True).start()
 
+    halo_keep = pltpu.make_async_copy(behind, halo_ref, in_sems.at[2])
+    ids_keep = pltpu.make_async_copy(ids_ref, ids_out, in_sems.at[1])
+
     @pl.when(step == 0)
     def _():
-        loads = [
-            pltpu.make_async_copy(qkv_hbm, qkv_ref, in_sems.at[0]),
-            pltpu.make_async_copy(ids_hbm, ids_ref, in_sems.at[1]),
-        ]
-        for load in loads:
-            load.start()
+        load = pltpu.make_async_copy(qkv_hbm, qkv_ref, in_sems.at[0])
+        load.start()
         barrier = pltpu.get_barrier_semaphore()
         for peer in at[1:]:
             pl.semaphore_signal(barrier, inc=1, device_id={"fsdp": peer}, device_id_type=MESH)
@@ -189,8 +188,13 @@
             p_near(r).start()
         w_copy(2, 1).start()
         w_keep(0).start()
-        for load in loads:
-            load.wait()
+        for s in range(seqs):
+            for i in range(row_ref.shape[2] // BLK):
+                span = slice(i * BLK, (i + 1) * BLK)
+                row = jnp.broadcast_to(row_ref[s, :, span].astype(jnp.float32), (128, BLK))
+                ids_ref[s, span, :] = row.T[:, 0:1].astype(jnp.int32)
+        ids_keep.start()
+        load.wait()
         for s in range(seqs):
             fill_keys(s, heads, qkv_ref, ids_ref, docs, WINDOW, keys, values, values_t, None)
 
@@ -204,7 +208,7 @@
         def _():
             behind[...] = jnp.zeros_like(behind)
 
-        halo_ref[...] = behind[...]
+        halo_keep.start()
         for s in range(seqs):
             fill_keys(s, heads, behind, ids_ref, docs, 0, keys, values, values_t, None)
 
@@ -229,7 +233,7 @@
         total = jnp.where(sub == HD + 1, peak, total).T
         norm = total[:, HD : HD + 1]
         part = (total[:, :HD] / norm).astype(low)
-        out_ref[seq, pl.ds(start, BLK), h * HD : (h + 1) * HD] = part
+        out_ref[0, :, h * HD : (h + 1) * HD] = part
         sent[step, :, h * HD : (h + 1) * HD] = part
         lse = total[:, HD + 1 : HD + 2] + jnp.log(norm)
         hi, mid, lo = split3(-lse)
@@ -237,7 +241,7 @@
         q2 = jnp.where(lane == lse_lane, hi, q2)
         q2 = jnp.where(lane == lse_lane + 1, mid, q2)
         q2 = jnp.where(lane == lse_lane + 2, lo, q2)
-        q2_ref[seq, h, pl.ds(start, BLK), :] = q2.astype(low)
+        q2_ref[0, h] = q2.astype(low)
 
     span = sent.shape[2]
 
@@ -289,6 +293,8 @@
             own(s).wait()
             for k in range(1, group):
                 away(s, k, at[k]).wait()
+        halo_keep.wait()
+        ids_keep.wait()
         w_keep(0).wait()
         for a in range(2):
             for r in (1, 2, 3, 4, 5):
@@ -341,30 +347,38 @@
                 keys_t[s * heads + h, :, span] = k.T
 
 
-def attend(qkv, ids, docs, out_w, fc_w, proj_w, heads, group):
+def attend(qkv, ids_row, docs, out_w, fc_w, proj_w, heads, group):
     seqs, rows, cols = qkv.shape
-    ext = ids.shape[1]
+    ext = ids_row.shape[2]
     assert rows // BLK == group
     low = jnp.bfloat16
     vmem = pl.BlockSpec(memory_space=pltpu.VMEM)
     hbm = pl.BlockSpec(memory_space=pl.ANY)
     every = seqs * heads
+    half = group // 2
+    seq_of = lambda i: lax.rem(lax.div(i, half), 2)
+    place_of = lambda i: (1 - lax.div(i, group)) * half + lax.rem(i + lax.axis_index("fsdp"), half)
     return pl.pallas_call(
         functools.partial(attend_kernel, heads, group, docs),
         grid=(seqs * rows // BLK,),
-        in_specs=[hbm] * 5,
-        out_specs=[vmem] * 3 + [hbm] * 4,
+        in_specs=[hbm, vmem] + [hbm] * 3,
+        out_specs=[
+            pl.BlockSpec((1, BLK, heads * HD), lambda i: (seq_of(i), place_of(i), 0)),
+            pl.BlockSpec((1, heads, BLK, 2 * HD), lambda i: (seq_of(i), 0, place_of(i), 0)),
+        ]
+        + [hbm] * 6,
         out_shape=[
             jax.ShapeDtypeStruct((seqs, rows, heads * HD), low),
             jax.ShapeDtypeStruct((seqs, heads, rows, 2 * HD), low),
             jax.ShapeDtypeStruct((seqs, WINDOW, heads * 2 * HD), low),
             jax.ShapeDtypeStruct((seqs, BLK, group * heads * HD), low),
         ]
-        + [jax.ShapeDtypeStruct((n,) + w.shape, low) for n, w in ((group, out_w), (NEAR - 1, fc_w), (NEAR - 1, proj_w))],
+        + [jax.ShapeDtypeStruct((n,) + w.shape, low) for n, w in ((group, out_w), (NEAR - 1, fc_w), (NEAR - 1, proj_w))]
+        + [jax.ShapeDtypeStruct((seqs, ext, 1), jnp.int32)],
         scratch_shapes=[
             pltpu.VMEM(qkv.shape, low),
-            pltpu.VMEM(ids.shape, jnp.int32),
-            pltpu.SemaphoreType.DMA((2,)),
+            pltpu.VMEM((seqs, ext, 1), jnp.int32),
+            pltpu.SemaphoreType.DMA((3,)),
             pltpu.VMEM((every, ext, 2 * HD), low),
             pltpu.VMEM((every, ext, 2 * HD), low),
             pltpu.VMEM((every, 2 * HD, ext), low),
@@ -380,7 +394,7 @@
         ],
         compiler_params=pltpu.CompilerParams(vmem_limit_bytes=56 * 2**20, collective_id=1, has_side_effects=True),
         name="attend",
-    )(qkv, ids, out_w, fc_w, proj_w)
+    )(qkv, ids_row, out_w, fc_w, proj_w)
 
 
 def mask_features(segment_ext, docs):
@@ -401,8 +415,8 @@
 
 
 def project_kernel(
-    x_ref, parts, w_ref, b_ref, all_small_ref, pieces_out, qkv_ref,
-    z1, pieces, smalls, small_ref, small_send, small_recv, send_sems, recv_sems, out_sems,
+    x_ref, parts, w_ref, b_ref, all_small_ref, pieces_out, qkv_out,
+    qkv_ref, give_sems, z1, pieces, smalls, small_ref, small_send, small_recv, send_sems, recv_sems, out_sems,
 ):
     group = all_small_ref.shape[0]
     me = lax.axis_index("fsdp")
@@ -444,6 +458,10 @@
     def keep(k, s):
         return pltpu.make_async_copy(chunk(at[k], s), pieces_out.at[s, pl.ds(pl.multiple_of(at[k] * rows, rows), rows)], out_sems.at[k, s])
 
+    def give(k, s):
+        span = pl.ds(pl.multiple_of(at[k] * rows, rows), rows)
+        return pltpu.make_async_copy(qkv_ref.at[s, span], qkv_out.at[s, span], give_sems.at[k, s])
+
     def project(k, s):
         keep(k, s).start()
         start = pl.multiple_of(at[k] * rows, rows)
@@ -451,6 +469,7 @@
         head = [made[:, h * 3 * HD : (h + 1) * 3 * HD] for h in range(heads)]
         made = jnp.concatenate([h[:, HD:] for h in head] + [h[:, :HD] for h in head], axis=1)
         qkv_ref[s, pl.ds(start, rows), :] = made
+        give(k, s).start()
 
     z1[...] = standardize(x_ref[:rows, :].astype(f32))[0]
     for k in range(1, group):
@@ -502,6 +521,7 @@
             move(r, s).wait_send()
         for k in range(group):
             keep(k, s).wait()
+            give(k, s).wait()
 
 
 def gather_project(x, smalls, weight, bias, group):
@@ -514,13 +534,15 @@
     return pl.pallas_call(
         gather_project_kernel,
         in_specs=[vmem] * 10,
-        out_specs=[vmem, pl.BlockSpec(memory_space=pl.ANY), vmem],
+        out_specs=[vmem, pl.BlockSpec(memory_space=pl.ANY), pl.BlockSpec(memory_space=pl.ANY)],
         out_shape=[
             jax.ShapeDtypeStruct((group, 16, span), low),
             jax.ShapeDtypeStruct((2, group * half, width), low),
             jax.ShapeDtypeStruct((2, group * half, cols), low),
         ],
         scratch_shapes=[
+            pltpu.VMEM((2, group * half, cols), low),
+            pltpu.SemaphoreType.DMA((group, 2)),
             pltpu.VMEM((half, width), jnp.float32),
             pltpu.VMEM((group, 2, half, width), low),
             pltpu.VMEM((group, 16, span), low),
@@ -532,7 +554,7 @@
             pltpu.SemaphoreType.DMA((group, 2)),
         ],
         compiler_params=pltpu.CompilerParams(
-            vmem_limit_bytes=48 * 2**20, collective_id=2, has_side_effects=True
+            vmem_limit_bytes=60 * 2**20, collective_id=2, has_side_effects=True
         ),
         name="gather_project",
     )(x, *smalls, weight, bias)
@@ -696,41 +718,6 @@
     ghidden = ghidden.astype(low)
     total[...] += nn(active, proj_w[here])
     gnormed[...] += nt(ghidden, fc_w[here])
-    given[fresh, 0] = tn(normed[...], ghidden).astype(low)
-    gproj = tn(active, cot_ref[...]).astype(low)
-    size, part = gproj.shape[0], fc_w.shape[2]
-    for i in range(gproj.shape[1] // part):
-        given[fresh, 1, i * size : (i + 1) * size, :] = gproj[:, i * part : (i + 1) * part]
-
-    @pl.when(odd == 0)
-    def _():
-        pair_copy(j).start()
-
-    @pl.when(odd == 1)
-    def _():
-        pair_copy(j).wait_recv()
-
-        def add(i, _):
-            part = pl.ds(pl.multiple_of(lax.rem(i, 8) * 128, 128), 128)
-            a = lax.div(i, 8)
-            taken[j, a, part, :] = (taken[j, a, part, :].astype(f32) + given[2, a, part, :].astype(f32)).astype(low)
-            return 0
-
-        lax.fori_loop(0, 16, add, 0)
-        keep_copy(j).start()
-
-    for a in range(2):
-        @pl.when(step == 1 + 2 * a)
-        def _(a=a):
-            side_copy(a).start()
-
-    @pl.when(step == 3)
-    def _():
-        for a in range(2):
-            far_copy(a, 0).wait_recv()
-            far_copy(a, 1).wait_recv()
-            far_copy(a, 2).start()
-
     @pl.when(step == last)
     def _():
         cot32 = cot_ref[...].astype(f32)
@@ -743,6 +730,46 @@
             gmerged[s] = back[s * block : (s + 1) * block, :]
         for k in (6, 2, 4, 3, 5, 7, 1, 0):
             head_copy(k).start()
+
+    given[fresh, 0] = tn(normed[...], ghidden).astype(low)
+    gproj = tn(active, cot_ref[...]).astype(low)
+    size, part = gproj.shape[0], fc_w.shape[2]
+    for i in range(gproj.shape[1] // part):
+        given[fresh, 1, i * size : (i + 1) * size, :] = gproj[:, i * part : (i + 1) * part]
+
+    @pl.when(odd == 0)
+    def _():
+        pair_copy(j).start()
+
+    @pl.when(odd == 1)
+    def _():
+        pair_copy(j).wait_recv()
+
+        def add(i, _):
+            part = pl.ds(pl.multiple_of(lax.rem(i, 8) * 128, 128), 128)
+            a = lax.div(i, 8)
+            taken[j, a, part, :] = (taken[j, a, part, :].astype(f32) + given[2, a, part, :].astype(f32)).astype(low)
+            return 0
+
+        lax.fori_loop(0, 16, add, 0)
+        keep_copy(j).start()
+
+    for a in range(2):
+        @pl.when(step == 1 + 2 * a)
+        def _(a=a):
+            side_copy(a).start()
+
+    @pl.when(step == 3)
+    def _():
+        for a in range(2):
+            far_copy(a, 0).wait_recv()
+            far_copy(a, 1).wait_recv()
+            far_copy(a, 2).start()
+
+    @pl.when(step == last)
+    def _():
+        gattn = gres_ref[...].astype(low)
+        g, z = gnormed[...], z2[...]
         gout = tn(merged_ref[...], gattn)
         for k in range(1, group, 2):
             gout_given[k // 2] = gout[k * span : (k + 1) * span, :].astype(low)
@@ -751,7 +778,7 @@
         gvec_ref[0:1, :] = column_sums(gattn.astype(f32))
         gvec_ref[1:2, :] = column_sums(g * z)
         gvec_ref[2:3, :] = column_sums(g)
-        gvec_ref[3:4, :] = column_sums(cot32)
+        gvec_ref[3:4, :] = column_sums(cot_ref[...].astype(f32))
         gout_copy().wait_recv()
         for k in range(0, group, 2):
             mine = gout[k * span : (k + 1) * span, :].astype(low).astype(f32)
@@ -1762,12 +1789,11 @@
     smalls = [v.reshape(-1, shard) for v in smalls]
     padded_ids = jnp.concatenate([jnp.full((seqs, WINDOW), -1, jnp.int32), segment_ids], axis=1)
     segment_ext = lax.dynamic_slice_in_dim(padded_ids, seq_index * part_rows, WINDOW + part_rows, 1)
-    ids = segment_ext[..., None]
     x = inputs.reshape(seqs * local_rows, width)
     cot = cotangent.reshape(seqs * local_rows, width)
     all_small, z1, qkv = gather_project(x, smalls, qkv_weight, qv_bias, group)
-    head_out, q2, halo, merged, out_all, fc_near, proj_near = attend(
-        qkv, ids, docs, out_weight, fc_weight, proj_weight, heads, group
+    head_out, q2, halo, merged, out_all, fc_near, proj_near, ids = attend(
+        qkv, segment_ext[:, None], docs, out_weight, fc_weight, proj_weight, heads, group
     )
     layer_output, g_resid, g_heads, kept, side, out_kept, gvec, gfcb = feed_forward(
         x, cot, merged.reshape(x.shape), out_all.reshape(width, width), fc_near, proj_near, fc_weight, proj_weight, all_small

time: 346 us -> 343 us (level)
  local copies, waits for them, and re-layouts: 9.43 us -> 5.36 us
where the time goes in v3:
time: 343 us; the launch traced here: 337 us
  Pallas kernels  323 us (94%)
  other arithmetic  7.51 us (2%)
  local copies, waits for them, and re-layouts  5.36 us (2%)
    pallas_call x1, Pallas kernels, finish(): pl.pallas_call(finish_kernel, in_specs=[hbm] * 4 + [vmem, hbm, hbm, vmem,...  90.8 us
    pallas_call x1, Pallas kernels, feed_forward(): pl.pallas_call(functools.partial(feed_forward_kernel, group), grid=(group...  67.1 us
    pallas_call x1, Pallas kernels, attend(): pl.pallas_call(functools.partial(attend_kernel, heads, group, docs), grid...  59.9 us
    pallas_call x1, Pallas kernels, attend_back(): pl.pallas_call(functools.partial(attend_back_kernel, heads, group, docs),...  56.1 us
    pallas_call x1, Pallas kernels, gather_project(): pl.pallas_call(gather_project_kernel, in_specs=[vmem] * 10, out_specs=[vm...  49.4 us

profile of v3, /device:TPU:0, one launch (start us, length us, event | category | flops | bytes accessed | tf_op | source)
XLA Modules:
  0.0 337.2 jit_solution(12143256858109970000)
XLA Ops:
  0.6 0.7 pad_dynamic-slice_fusion
  1.4 0.6 broadcast_in_dim.4.row_ref
  2.0 49.4 %gather_project.1 = (bf16[8,16,128]{2,1,0:T(8,128)(2,1)}, bf16[2,2048,1024]{2,1,0:T(8,128)(2,1)}, bf16[2,2048,384]{2,1,0:T(8,128)(2,1)}) custom-call(bf16[512,1024]{1,0:T(8,128)(2,1)} %bitcast.32, bf16[1,128]{1,0:T(2,128)(2,1)} %bitcast.45, bf16[1,128]{1,0:T(2,128)(2,1)} %bitcast.46, bf16[1,128]{1,0:T(2,128)(2,1)} %bitcast.47, bf16[1,128]{1,0:T(2,128)(2,1)} %bitcast.48, ...), custom_call_target="tpu_custom_call" | custom-call | tf_op jit(solution)/shard_map/gather_project/pallas_call | solution.py:534
  51.5 59.9 %attend.1 = (bf16[2,2048,128]{2,1,0:T(8,128)(2,1)}, bf16[2,2,2048,128]{3,2,1,0:T(8,128)(2,1)}, bf16[2,1024,256]{2,1,0:T(8,128)(2,1)}, bf16[2,256,1024]{2,1,0:T(8...) custom-call(bf16[2,2048,384]{2,1,0:T(8,128)(2,1)} %get-tuple-element, ...), custom_call_target="tpu_custom_call" | custom-call | tf_op jit(solution)/shard_map/attend/pallas_call | solution.py:361
  111.4 67.1 %feed_forward.1 = (bf16[512,1024]{1,0:T(8,128)(2,1)}, f32[512,1024]{1,0:T(8,128)}, bf16[2,2048,128]{2,1,0:T(8,128)(2,1)}, bf16[4,2,1024,512]{3,2,1,0:T(8,128)(2,...) custom-call(bf16[512,1024]{1,0:T(8,128)(2,1)} %bitcast.33, ...), custom_call_target="tpu_custom_call" | custom-call | tf_op jit(solution)/shard_map/feed_forward/pallas_call | solution.py:807
  178.5 0.0 copy-start
  178.5 56.1 %attend_back.1 = (bf16[2,2048,384]{2,1,0:T(8,128)(2,1)}, bf16[2,1024,512]{2,1,0:T(8,128)(2,1)}) custom-call(bf16[2,2048,384]{2,1,0:T(8,128)(2,1)} %get-tuple-element.41.qkv_hbm, bf16[2,1024,256]{2,1,0:T(8,128)(2,1)} %get-tuple-element.48.halo_hbm, s32[2,3072,1]{2,1,0:T(8,128)} %get-tuple-element.49.ids_hbm, ...), custom_call_target="tpu_custom_call" | custom-call | tf_op jit(solution)/shard_map/attend_back/pallas_call | solution.py:1060
  234.6 0.0 copy-done
  234.6 0.3 copy.31
  235.0 0.9 maximum_bitcast_fusion.wt_hbm
  235.9 90.8 %finish.1 = (bf16[512,1024]{1,0:T(8,128)(2,1)}, bf16[1024,512]{1,0:T(8,128)(2,1)}, bf16[512,1024]{1,0:T(8,128)(2,1)}, bf16[128,1024]{1,0:T(8,128)(2,1)}, bf16[1024,384]{1,0:T(8,128)(2,1)}, /*index=5*/f32[16,128]{1,0:T(8,128)}) custom-call(bf16[2,2048,384]{2,1,0:T(8,128)(2,1)} %get-tuple-element.55.g_hbm, bf16[384,1024]{1,0:T(8,128)(2,1)} %maximum_bitcast_fusion.wt_hbm, ...), custom_call_target="tpu_custom_call" | custom-call | tf_op jit(solution)/shard_map/finish/pallas_call | solution.py:1427
  326.7 0.0 copy-start.1
  326.7 2.9 convert_element_type.14
  329.7 0.0 copy-done.1
  329.7 1.6 convert_element_type.15
  331.2 0.0 copy-done.4
  331.2 1.2 convert_element_type.12
  332.5 0.0 copy-done.5
  332.5 0.8 convert_element_type.13
  333.3 0.5 slice_bitcast_fusion.1
  333.9 0.6 slice_bitcast_fusion
  334.4 0.6 slice.34
  335.0 1.0 copy.34
  336.0 1.0 copy.35
  (10 shorter events, 0.1 us)
Async XLA Ops:
  178.5 56.1 %copy-start = (bf16[1024,384]{1,0:T(8,128)(2,1)S(1)}, bf16[1024,384]{1,0:T(8,128)(2,1)}, u32[]{:S(2)}) copy-start(bf16[1024,384]{1,0:T(8,128)(2,1)} %rest_7_.1) | copy-start | bytes 2359300
  326.7 2.9 copy-start.1
  329.7 1.6 copy-start.4
  329.7 2.8 copy-start.5
  331.2 2.1 copy-start.6
  331.2 3.8 %copy-start.2 = (bf16[512,1024]{1,0:T(8,128)(2,1)S(1)}, bf16[512,1024]{1,0:T(8,128)(2,1)}, u32[]{:S(2)}) copy-start(bf16[512,1024]{1,0:T(8,128)(2,1)} %get-tuple-element.47) | copy-start | bytes 3145732
  331.2 4.8 %copy-start.3 = (bf16[512,1024]{1,0:T(8,128)(2,1)S(1)}, bf16[512,1024]{1,0:T(8,128)(2,1)}, u32[]{:S(2)}) copy-start(bf16[512,1024]{1,0:T(8,128)(2,1)} %get-tuple-element.62) | copy-start | bytes 3145732
